TPU v7x, 512 devices: a whole 4x4x16 slice. The times are simulated.
512 devices in a mesh: group: 32 (over z, core), row: 16 (over x, y).
Axes of the slice: x: 4, y: 4, z: 16, core: 2. Of those that a mesh axis runs over, the one named last changes fastest.
Arguments:
- queries: bfloat16 [64, 16, 64, 2560], P('group', 'row'), may hold values from -5 to 5
- keys: bfloat16 [64, 16, 64, 2560], P('group', 'row'), may hold values from -5 to 5
- values: bfloat16 [64, 16, 64, 2560], P('group', 'row'), may hold values from -6 to 6
- out_grad: bfloat16 [64, 16, 64, 2560], P('group', 'row'), may hold values from -6 to 6
- slots: int32 [64, 16, 64], P('group', 'row'), may hold values from 0 to 7
- decay: float32 [20], replicated, may hold values from 0.3 to 0.95
Outputs:
- query_grad: bfloat16 [64, 16, 64, 2560], P('group', 'row')
- key_grad: bfloat16 [64, 16, 64, 2560], P('group', 'row')
- value_grad: bfloat16 [64, 16, 64, 2560], P('group', 'row')
All inputs are finite; a program needn't handle non-finite values.
Results may differ from a plain program's by a relative error of at most 0.025.
Values may be sent and summed in bfloat16 or wider, within the bound.
A program may use at most 128 MiB of HBM per device.

v0:
```python
import jax
import jax.numpy as jnp
from jax import lax
from jax.sharding import PartitionSpec as P

S = 8


def from_behind(array, axis, by):
    count = lax.axis_size(axis)
    pairs = [(i, i + by) for i in range(count) if 0 <= i + by < count]
    return lax.ppermute(array, axis, pairs)


def extended(block, sides, width):
    for axis, dim in sides:
        count = lax.axis_size(axis)
        forward = [(i, i + 1) for i in range(count - 1)]
        backward = [(target, source) for source, target in forward]
        low = lax.ppermute(
            lax.slice_in_dim(block, block.shape[dim] - width, None, axis=dim), axis, forward
        )
        high = lax.ppermute(lax.slice_in_dim(block, 0, width, axis=dim), axis, backward)
        block = jnp.concatenate([low, block, high], axis=dim)
    return block


def attend(queries, keys, values, valid, grads):
    scale = queries.shape[-1] ** (-0.5)
    scores = (
        jnp.einsum("bqhe,bkhe->bhqk", queries, keys, preferred_element_type=jnp.float32) * scale
    )
    scores = jnp.where(valid[:, None, None, :], scores, -1e30)
    top = jnp.max(scores, axis=-1, keepdims=True)
    weights = jnp.exp(scores - top)
    total = jnp.sum(weights, axis=-1, keepdims=True)
    probs = weights / total
    probs_b = probs.astype(jnp.bfloat16)
    output = jnp.einsum("bhqk,bkhe->bqhe", probs_b, values, preferred_element_type=jnp.float32)
    delta = jnp.einsum("bqhe,bqhe->bhq", grads.astype(jnp.float32), output)
    dprob = jnp.einsum("bqhe,bkhe->bhqk", grads, values, preferred_element_type=jnp.float32)
    dscore = (probs * (dprob - delta[..., None]) * scale).astype(jnp.bfloat16)
    dq = jnp.einsum("bhqk,bkhe->bqhe", dscore, keys, preferred_element_type=jnp.float32)
    dk = jnp.einsum("bhqk,bqhe->bkhe", dscore, queries, preferred_element_type=jnp.float32)
    dv = jnp.einsum("bhqk,bqhe->bkhe", probs_b, grads, preferred_element_type=jnp.float32)
    stats = jnp.stack([top[..., 0], total[..., 0], delta])
    return (dq, dk, dv, stats)


def carry_forward(rate, stacked):

    def advance(step, state):
        return from_behind(rate * state + stacked, "group", 1)

    return lax.fori_loop(0, lax.axis_size("group") - 1, advance, jnp.zeros_like(stacked))


def carry_backward(rate, stacked):

    def advance(step, state):
        return from_behind((rate * state + stacked).astype(jnp.bfloat16), "group", -1).astype(
            jnp.float32
        )

    return lax.fori_loop(0, lax.axis_size("group") - 1, advance, jnp.zeros_like(stacked))


def stripe_total(stacked):
    return lax.psum(stacked.astype(jnp.bfloat16), "row").astype(jnp.float32)


def per_device(queries, keys, values, out_grad, slots, decay):
    frames, _, width, feats = queries.shape
    half = feats // 2
    heads = decay.shape[0]
    size = feats // heads
    paired = heads // 2
    stripes = lax.axis_size("row")
    position = lax.axis_index("row")
    tokens = frames * width
    slot_ids = jnp.arange(S, dtype=jnp.int32)
    member = slots.reshape(tokens, 1) == slot_ids[None, :]
    member_b = member.astype(jnp.bfloat16)
    member_f = member.astype(jnp.float32)
    sum_k = jnp.dot(member_b.T, keys.reshape(tokens, feats), preferred_element_type=jnp.float32)
    sum_v = jnp.dot(member_b.T, values.reshape(tokens, feats), preferred_element_type=jnp.float32)
    counts = jnp.sum(member_f, axis=0)
    sum_k, sum_v, counts = lax.psum((sum_k, sum_v, counts), "row")
    inv_norm = 1.0 / jnp.sqrt(jnp.maximum(counts, 1.0))
    pooled = jnp.stack([sum_k * inv_norm[:, None], sum_v * inv_norm[:, None]])
    rate = jnp.repeat(decay, size)
    memory = carry_forward(rate, pooled).astype(jnp.bfloat16)
    col_q, col_k, col_v, col_g = (
        lax.all_to_all(queries[..., half:], "row", split_axis=2, concat_axis=1, tiled=True),
        lax.all_to_all(keys[..., half:], "row", split_axis=2, concat_axis=1, tiled=True),
        lax.all_to_all(values[..., half:], "row", split_axis=2, concat_axis=1, tiled=True),
        lax.all_to_all(out_grad[..., half:], "row", split_axis=2, concat_axis=1, tiled=True),
    )
    stripe_shape = (frames, 1, width, half)
    both_q = jnp.stack(
        [queries[..., :half].reshape(tokens, paired, size), col_q.reshape(tokens, paired, size)]
    )
    both_g = jnp.stack(
        [out_grad[..., :half].reshape(tokens, paired, size), col_g.reshape(tokens, paired, size)]
    )
    local_kv = jnp.stack(
        [
            keys[..., :half],
            values[..., :half],
            col_k.reshape(stripe_shape),
            col_v.reshape(stripe_shape),
        ]
    )
    beside_all = extended(local_kv, (("row", 2),), 1)
    nk = frames * 3 * width
    mem_k = jnp.stack([memory[0][:, :half], memory[0][:, half:]]).reshape(2, S, paired, size)
    mem_v = jnp.stack([memory[1][:, :half], memory[1][:, half:]]).reshape(2, S, paired, size)
    win_k = jnp.stack([beside_all[0], beside_all[2]]).reshape(2, nk, paired, size)
    win_v = jnp.stack([beside_all[1], beside_all[3]]).reshape(2, nk, paired, size)
    all_k = jnp.concatenate([win_k, mem_k], axis=1)
    all_v = jnp.concatenate([win_v, mem_v], axis=1)
    flags = jnp.stack([position > 0, position >= 0, position < stripes - 1])
    window_valid = jnp.broadcast_to(flags[None, :, None], (frames, 3, width)).reshape(nk)
    valid = jnp.concatenate([window_valid, jnp.ones((S,), dtype=bool)])
    valid = jnp.broadcast_to(valid[None, :], (2, nk + S))
    dq, dk, dv, stats = attend(both_q, all_k, all_v, valid, both_g)
    dk_win = dk[:, :nk].reshape(2, frames, 3, width, half)
    dv_win = dv[:, :nk].reshape(2, frames, 3, width, half)
    rims = jnp.stack([dk_win[0], dv_win[0], dk_win[1], dv_win[1]])
    from_above = from_behind(rims[:, :, 0].astype(jnp.bfloat16), "row", -1).astype(jnp.float32)
    from_below = from_behind(rims[:, :, 2].astype(jnp.bfloat16), "row", 1).astype(jnp.float32)
    own = rims[:, :, 1] + from_above + from_below
    dmem_k = jnp.concatenate([dk[0, nk:].reshape(S, half), dk[1, nk:].reshape(S, half)], axis=1)
    dmem_v = jnp.concatenate([dv[0, nk:].reshape(S, half), dv[1, nk:].reshape(S, half)], axis=1)
    dmem = jnp.stack([dmem_k, dmem_v])
    dpool = carry_backward(rate, stripe_total(dmem))
    add_k = jnp.dot(member_f, dpool[0] * inv_norm[:, None], precision=lax.Precision.HIGHEST)
    add_v = jnp.dot(member_f, dpool[1] * inv_norm[:, None], precision=lax.Precision.HIGHEST)
    col_shape = (frames, stripes, width // stripes, half)
    back_q, back_k, back_v = (
        lax.all_to_all(dq[1].reshape(col_shape), "row", split_axis=1, concat_axis=2, tiled=True),
        lax.all_to_all(own[2].reshape(col_shape), "row", split_axis=1, concat_axis=2, tiled=True),
        lax.all_to_all(own[3].reshape(col_shape), "row", split_axis=1, concat_axis=2, tiled=True),
    )
    row_shape = (frames, 1, width, half)
    full_shape = (frames, 1, width, feats)
    query_grad = jnp.concatenate([dq[0].reshape(row_shape), back_q], axis=-1).astype(jnp.bfloat16)
    key_grad = (
        jnp.concatenate([own[0].reshape(row_shape), back_k], axis=-1) + add_k.reshape(full_shape)
    ).astype(jnp.bfloat16)
    value_grad = (
        jnp.concatenate([own[1].reshape(row_shape), back_v], axis=-1) + add_v.reshape(full_shape)
    ).astype(jnp.bfloat16)
    return (query_grad, key_grad, value_grad)


def solution(mesh):
    return jax.shard_map(
        per_device,
        mesh=mesh,
        in_specs=(
            P("group", "row", None, None),
            P("group", "row", None, None),
            P("group", "row", None, None),
            P("group", "row", None, None),
            P("group", "row", None),
            P(),
        ),
        out_specs=(
            P("group", "row", None, None),
            P("group", "row", None, None),
            P("group", "row", None, None),
        ),
        check_vma=False,
    )
```

profile of v0, /device:TPU:101, one launch (start us, length us, event | category | flops | bytes accessed | tf_op | source)
XLA Modules:
  0.0 948.8 jit_solution(12148729714318797530)
XLA Ops:
  9.5 6.9 all-to-all-start
  19.6 26.1 %psum.29 = f32[8]{0:T(128)S(1)} all-reduce(f32[8]{0:T(128)S(1)} %convert_reduce_fusion), channel_id=1, replica_groups=mesh['group'=32,'row'=16] {'row'}, use_global_device_ids=true, to_apply=%region_2.0 | all-reduce | flops 8 | bytes 64 | tf_op jit(solution)/shard_map/psum | solution.py:88
  52.3 83.3 %all-reduce.7.cloned.1.call-done = (f32[8,2560]{1,0:T(8,128)}, f32[8,2560]{1,0:T(8,128)}) async-done(((f32[8,2560]{1,0:T(8,128)}, f32[8,2560]{1,0:T(8,128)}), (f32[8,2560]{1,0:T(8,128)}, f32[8,2560]{1,0:T(8,128)})) %all-reduce.7.cloned.1.call-update) | async-done | bytes 163856 | tf_op jit(solution)/shard_map/psum | solution.py:88
  136.6 5.7 all-to-all-start.1
  142.3 248.0 %while.22 = (s32[]{:T(128)}, f32[2,8,2560]{2,1,0:T(8,128)S(1)}, f32[2,8,2560]{2,1,0:T(8,128)S(1)}, f32[20]{0:T(128)S(1)}, s32[]{:T(128)}) while((s32[]{:T(128)}, f32[2,8,2560]{2,1,0:T(8,128)S(1)}, f32[2,8,2560]{2,1,0:T(8,128)S(1)}, f32[20]{0:T(128)S(1)}, s32[]{:T(128)}) %tuple.82), condition=%wide.region_5.0_spmd.clone, body=%wide.region_4.0_spmd.clone.sunk | while | flops 81922 | bytes 1167541 | solution.py:55
  142.4 7.2 collective-permute-start
  152.0 5.6 collective-permute-start
  159.9 5.6 collective-permute-start
  167.8 5.6 collective-permute-start
  175.8 5.6 collective-permute-start
  183.7 5.6 collective-permute-start
  191.7 5.6 collective-permute-start
  199.6 5.6 collective-permute-start
  207.6 5.6 collective-permute-start
  215.5 5.6 collective-permute-start
  223.5 5.6 collective-permute-start
  231.4 5.6 collective-permute-start
  239.4 5.6 collective-permute-start
  247.3 5.6 collective-permute-start
  255.3 5.6 collective-permute-start
  263.2 5.6 collective-permute-start
  271.2 5.6 collective-permute-start
  279.1 5.6 collective-permute-start
  287.1 5.6 collective-permute-start
  295.0 5.6 collective-permute-start
  303.0 5.6 collective-permute-start
  310.9 5.6 collective-permute-start
  318.8 5.6 collective-permute-start
  326.8 5.6 collective-permute-start
  334.7 5.6 collective-permute-start
  342.7 5.6 collective-permute-start
  350.6 5.6 collective-permute-start
  358.6 5.6 collective-permute-start
  366.5 5.6 collective-permute-start
  374.5 5.6 collective-permute-start
  382.4 5.6 collective-permute-start
  390.3 6.7 all-to-all-start.2
  406.8 8.1 all-to-all-start.3
  416.0 26.0 %all-to-all-done.3 = bf16[2,1,64,1280]{3,0,1,2:T(2,128)(2,1)S(1)} async-done(((bf16[2,1,64,1280]{3,0,1,2:T(2,128)(2,1)}), bf16[2,1,64,1280]{3,0,1,2:T(2,128)(2,1)S(1)}, u32[]{:S(2)}, u32[]{:S(2)}) %all-to-all-start.3) | async-done | bytes 327712 | tf_op jit(solution)/shard_map/all_to_all | solution.py:97
  447.0 8.8 pad_maximum_fusion.1
  538.5 7.5 all-to-all-start.4
  547.4 17.0 %collective-permute-done.4 = bf16[4,2,64,1280]{3,2,1,0:T(8,128)(2,1)} collective-permute-done((bf16[4,2,64,1280]{3,2,1,0:T(8,128)(2,1)}, bf16[4,2,64,1280]{3,2,1,0:T(8,128)(2,1)}, u32[]{:S(2)}, u32[]{:S(2)}) %collective-permute-start.4) | collective-permute-done | bytes 1310752 | tf_op jit(solution)/shard_map/ppermute | solution.py:12
  582.2 7.1 all-to-all-done.6
  589.3 6.1 all-to-all-start.5
  596.9 111.4 %all-reduce.5.cloned.1.call-done = bf16[2,8,2560]{2,1,0:T(8,128)(2,1)} async-done(((bf16[2,8,2560]{2,1,0:T(8,128)(2,1)}), bf16[2,8,2560]{2,1,0:T(8,128)(2,1)}) %all-reduce.5.cloned.1.call-update) | async-done | bytes 81936 | tf_op jit(solution)/shard_map/psum | solution.py:69
  716.7 221.9 %while.23 = (s32[]{:T(128)}, f32[2,8,2560]{2,1,0:T(8,128)S(1)}, f32[2,8,2560]{2,1,0:T(8,128)S(1)}, f32[20]{0:T(128)S(1)}, s32[]{:T(128)}, /*index=5*/s32[]{:T(128)}) while((s32[]{:T(128)}, f32[2,8,2560]{2,1,0:T(8,128)S(1)}, f32[2,8,2560]{2,1,0:T(8,128)S(1)}, f32[20]{0:T(128)S(1)}, s32[]{:T(128)}, /*index=5*/s32[]{:T(128)}) %tuple.83), condition=%wide.region_10.11_spmd.clone, body=%wide.region_9.10_spmd.clone.sunk | while | flops 204803 | bytes 1003719 | solution.py:65
  763.1 5.0 collective-permute-done.1
  770.2 5.0 collective-permute-done.1
  (386 shorter events, 426.6 us)
Async XLA Ops:
  9.5 127.0 %all-to-all-start = ((bf16[2,1,64,1280]{3,0,1,2:T(2,128)(2,1)}), bf16[2,1,64,1280]{3,0,1,2:T(2,128)(2,1)S(1)}, u32[]{:S(2)}, u32[]{:S(2)}) async-start(bf16[2,1,64,1280]{3,0,1,2:T(2,128)(2,1)} %copy.154), calls=%async_computation | async-start | bytes 655360 | tf_op jit(solution)/shard_map/all_to_all | solution.py:95
  16.4 119.1 %all-reduce.7.cloned.1.call-start = ((), (), s32[]{:S(2)}) async-start(), calls=%async_computation.8 | async-start | bytes 327680 | tf_op jit(solution)/shard_map/psum | solution.py:88
  136.6 253.7 %all-to-all-start.1 = ((bf16[2,1,64,1280]{3,0,1,2:T(2,128)(2,1)}), bf16[2,1,64,1280]{3,0,1,2:T(2,128)(2,1)S(1)}, u32[]{:S(2)}, u32[]{:S(2)}) async-start(bf16[2,1,64,1280]{3,0,1,2:T(2,128)(2,1)} %copy.155), calls=%async_computation.1 | async-start | bytes 655360 | tf_op jit(solution)/shard_map/all_to_all | solution.py:96
  142.4 9.5 collective-permute-start
  152.0 7.8 collective-permute-start
  159.9 7.8 collective-permute-start
  167.8 7.8 collective-permute-start
  175.8 7.8 collective-permute-start
  183.7 7.8 collective-permute-start
  191.7 7.8 collective-permute-start
  199.6 7.8 collective-permute-start
  207.6 7.8 collective-permute-start
  215.5 7.8 collective-permute-start
  223.5 7.8 collective-permute-start
  231.4 7.8 collective-permute-start
  239.4 7.8 collective-permute-start
  247.3 7.8 collective-permute-start
  255.3 7.8 collective-permute-start
  263.2 7.8 collective-permute-start
  271.2 7.8 collective-permute-start
  279.1 7.8 collective-permute-start
  287.1 7.8 collective-permute-start
  295.0 7.8 collective-permute-start
  303.0 7.8 collective-permute-start
  310.9 7.8 collective-permute-start
  318.8 7.8 collective-permute-start
  326.8 7.8 collective-permute-start
  334.7 7.8 collective-permute-start
  342.7 7.8 collective-permute-start
  350.6 7.8 collective-permute-start
  358.6 7.8 collective-permute-start
  366.5 7.8 collective-permute-start
  374.5 7.8 collective-permute-start
  382.4 7.8 collective-permute-start
  390.3 16.5 %all-to-all-start.2 = ((bf16[2,1,64,1280]{3,0,1,2:T(2,128)(2,1)}), bf16[2,1,64,1280]{3,0,1,2:T(2,128)(2,1)S(1)}, u32[]{:S(2)}, u32[]{:S(2)}) async-start(bf16[2,1,64,1280]{3,0,1,2:T(2,128)(2,1)} %copy.156), calls=%async_computation.2 | async-start | bytes 655360 | tf_op jit(solution)/shard_map/all_to_all | solution.py:94
  400.6 46.4 %collective-permute-start.3 = (bf16[4,2,1,64,1280]{4,1,3,2,0:T(2,128)(2,1)}, bf16[4,2,1,64,1280]{4,1,3,2,0:T(2,128)(2,1)}, u32[]{:S(2)}, u32[]{:S(2)}) collective-permute-start(bf16[4,2,1,64,1280]{4,1,3,2,0:T(2,128)(2,1)} %pad_maximum_fusion.4), channel_id=1, source_target_pairs={{1,0},{2,1},{3,2},{4,3},{5,4},{6,5},{7,6},{8,7},{9,8},{10,9},{11,1... | collective-permute-start | bytes 3932168 | tf_op jit(solution)/shard_map/ppermute | solution.py:23
  404.9 42.1 %collective-permute-start.2 = (bf16[4,2,1,64,1280]{4,1,3,2,0:T(2,128)(2,1)}, bf16[4,2,1,64,1280]{4,1,3,2,0:T(2,128)(2,1)}, u32[]{:S(2)}, u32[]{:S(2)}) collective-permute-start(bf16[4,2,1,64,1280]{4,1,3,2,0:T(2,128)(2,1)} %pad_maximum_fusion.4), channel_id=1, source_target_pairs={{0,1},{1,2},{2,3},{3,4},{4,5},{5,6},{6,7},{7,8},{8,9},{9,10},{10,1... | collective-permute-start | bytes 3932168 | tf_op jit(solution)/shard_map/ppermute | solution.py:20
  406.8 35.2 %all-to-all-start.3 = ((bf16[2,1,64,1280]{3,0,1,2:T(2,128)(2,1)}), bf16[2,1,64,1280]{3,0,1,2:T(2,128)(2,1)S(1)}, u32[]{:S(2)}, u32[]{:S(2)}) async-start(bf16[2,1,64,1280]{3,0,1,2:T(2,128)(2,1)} %copy.157), calls=%async_computation.3 | async-start | bytes 655360 | tf_op jit(solution)/shard_map/all_to_all | solution.py:97
  530.7 33.8 %collective-permute-start.4 = (bf16[4,2,64,1280]{3,2,1,0:T(8,128)(2,1)}, bf16[4,2,64,1280]{3,2,1,0:T(8,128)(2,1)}, u32[]{:S(2)}, u32[]{:S(2)}) collective-permute-start(bf16[4,2,64,1280]{3,2,1,0:T(8,128)(2,1)} %get-tuple-element.115), channel_id=1, source_target_pairs={{1,0},{2,1},{3,2},{4,3},{5,4},{6,5},{7,6},{8,7},{9,8},{10,9},{11,1... | collective-permute-start | bytes 3932168 | tf_op jit(solution)/shard_map/ppermute | solution.py:12
  532.6 36.1 %collective-permute-start.5 = (bf16[4,2,64,1280]{3,2,1,0:T(8,128)(2,1)}, bf16[4,2,64,1280]{3,2,1,0:T(8,128)(2,1)}, u32[]{:S(2)}, u32[]{:S(2)}) collective-permute-start(bf16[4,2,64,1280]{3,2,1,0:T(8,128)(2,1)} %get-tuple-element.116), channel_id=1, source_target_pairs={{0,1},{1,2},{2,3},{3,4},{4,5},{5,6},{6,7},{7,8},{8,9},{9,10},{10,1... | collective-permute-start | bytes 3932168 | tf_op jit(solution)/shard_map/ppermute | solution.py:12
  538.5 36.1 %all-to-all-start.4 = ((bf16[2,16,4,1280]{3,2,0,1:T(4,128)(2,1)}), bf16[2,16,4,1280]{3,2,0,1:T(4,128)(2,1)}, u32[]{:S(2)}, u32[]{:S(2)}) async-start(bf16[2,16,4,1280]{3,2,0,1:T(4,128)(2,1)} %copy.128), calls=%async_computation.4 | async-start | bytes 655360 | tf_op jit(solution)/shard_map/all_to_all | solution.py:141
  574.5 14.8 %all-to-all-start.6 = ((f32[2,16,4,1280]{3,2,0,1:T(4,128)}), f32[2,16,4,1280]{3,2,0,1:T(4,128)S(1)}, u32[]{:S(2)}, u32[]{:S(2)}) async-start(f32[2,16,4,1280]{3,2,0,1:T(4,128)} %copy.140), calls=%async_computation.6 | async-start | bytes 1310720 | tf_op jit(solution)/shard_map/all_to_all | solution.py:143
  589.3 124.1 %all-to-all-start.5 = ((f32[2,16,4,1280]{3,2,0,1:T(4,128)}), f32[2,16,4,1280]{3,2,0,1:T(4,128)}, u32[]{:S(2)}, u32[]{:S(2)}) async-start(f32[2,16,4,1280]{3,2,0,1:T(4,128)} %copy.138), calls=%async_computation.5 | async-start | bytes 1310720 | tf_op jit(solution)/shard_map/all_to_all | solution.py:142
  595.5 112.8 %all-reduce.5.cloned.1.call-start = ((), (), s32[]{:S(2)}) async-start(), calls=%async_computation.7 | async-start | bytes 163840 | tf_op jit(solution)/shard_map/psum | solution.py:69
  716.8 8.7 collective-permute-start.1
  761.1 7.0 collective-permute-start.1
  768.2 7.0 collective-permute-start.1
  775.3 7.0 collective-permute-start.1
  (41 other events, 390.6 us)
Sparse Core Ops, SparseCore 0:
  20.6 114.9 all-reduce.6
  600.1 108.1 all-reduce.4
where the time goes:
time: 958 us; the launch traced here: 949 us
  waiting for transfers between devices  474 us (49%)
  starting transfers between devices  294 us (31%)
  local copies, waits for them, and re-layouts  86.9 us (9%)
  other arithmetic  33.3 us (3%)
  blocking collectives  26.1 us (3%)
  matrix products  17.9 us (2%)
  between operations  14.8 us (2%)
    ppermute x64, waiting for transfers between devices, from_behind(): return lax.ppermute(array, axis, pairs)  246 us
    ppermute x64, starting transfers between devices, from_behind(): return lax.ppermute(array, axis, pairs)  242 us
    psum x1, waiting for transfers between devices, stripe_total(): return lax.psum(stacked.astype(jnp.bfloat16), 'row').astype(jnp.float32)  111 us
    psum x1, waiting for transfers between devices, per_device(): sum_k, sum_v, counts = lax.psum((sum_k, sum_v, counts), 'row')  83.3 us
    slice x10, local copies, waits for them, and re-layouts, per_device(): rims = jnp.stack([dk_win[0], dv_win[0], dk_win[1], dv_win[1]])  33.9 us
    psum x1, blocking collectives, per_device(): sum_k, sum_v, counts = lax.psum((sum_k, sum_v, counts), 'row')  26.1 us
    all_to_all x1, waiting for transfers between devices, per_device(): lax.all_to_all(out_grad[..., half:], 'row', split_axis=2, concat_axis=1,...  26 us
  transfers between devices with their start and end apart: 75, of which 68 were waited for; matrix products, arithmetic and copies ran while one was open for 4% of the time, Pallas kernels for 0%

commit v1 on v0

v1 whole, which is shorter than its diff:
```python
import jax
import jax.numpy as jnp
from jax import lax
from jax.experimental import pallas as pl
from jax.experimental.pallas import tpu as pltpu
from jax.sharding import PartitionSpec as P

S = 8
E = 128
TOKENS = 128
HALF = 1280
PART = 640
FEATS = 2560
ROWS = 16
MESH = pl.DeviceIdType.MESH
F32 = jnp.float32
BF16 = jnp.bfloat16
NEG = -1e30


def select(rows, cols, source):
    o = lax.broadcasted_iota(jnp.int32, (rows, cols), 0)
    i = lax.broadcasted_iota(jnp.int32, (rows, cols), 1)
    return jnp.where(source(o) == i, 1.0, 0.0).astype(BF16)


def select_back(rows, cols, source):
    i = lax.broadcasted_iota(jnp.int32, (rows, cols), 0)
    o = lax.broadcasted_iota(jnp.int32, (rows, cols), 1)
    return jnp.where(source(o) == i, 1.0, 0.0).astype(BF16)


def by_pair(s):
    return ((s >> 3) & 1) * 64 + (s >> 4) * 8 + (s & 7)


def by_stripe(o):
    return ((o >> 3) & 15) * 16 + ((o >> 2) & 1) * 8 + (o >> 7) * 4 + (o & 3)


def dot(a, b, ca=1, cb=0):
    return lax.dot_general(a, b, (((ca,), (cb,)), ((), ())), preferred_element_type=F32)


def unit(q, g, keys, values, low, high):
    scale = E ** (-0.5)
    s = dot(keys, q, 1, 1) * scale
    used = lax.broadcasted_iota(jnp.int32, (16, 128), 0) < S
    s = jnp.concatenate(
        [s[:128] + low, s[128:256], s[256:384] + high, jnp.where(used, s[384:], NEG)], axis=0
    )
    top = jnp.max(s, axis=0, keepdims=True)
    w = jnp.exp(s - top)
    p = w * (1.0 / jnp.sum(w, axis=0, keepdims=True))
    pb = p.astype(BF16)
    dprob = dot(values, g, 1, 1)
    delta = jnp.sum(pb.astype(F32) * dprob, axis=0, keepdims=True)
    ds = (p * ((dprob - delta) * scale)).astype(BF16)
    dk = dot(ds, q)
    dv = dot(pb, g)
    dq = dot(ds, keys, 0, 0)
    return dq, dk, dv


def kernel(
    q_ref, k_ref, v_ref, g_ref, slots_ref, decay_ref,
    oq_ref, ok_ref, ov_ref,
    ms, rs, zp, zb, bp, bt, mp, mem, memk, memv,
    ms2, rs2, zp2, zb2, bp2, bt2, mp2, mem2,
    m2, dm,
    cs, cr, sep, hr, hc, gs, gr, own, cown, cgs, cgr,
    bsq, bskv, brq, brkv,
    send, recv,
):
    r = lax.axis_index("row")
    n = lax.axis_index("group")
    blk = n // 8
    idx = n % 8
    x = r // 4
    y = r % 4
    hh = y % 2
    yh = y // 2
    jp = x + yh * (7 - 2 * x)

    def holder(pair, part):
        high = pair // 4
        low = pair % 4
        return (low + high * (3 - 2 * low)) * 4 + high * 2 + part

    def in_row(d):
        return lax.rem(r + d, ROWS)

    def in_block(d):
        return blk * 8 + lax.rem(idx + d, 8)

    def in_blocks(d):
        return lax.rem(blk + d, 4) * 8 + idx

    barrier = pltpu.get_barrier_semaphore()

    def greet(axis, pick, count):
        def body(d, c):
            pl.semaphore_signal(barrier, inc=1, device_id={axis: pick(d)}, device_id_type=MESH)
            return c

        lax.fori_loop(1, count, body, 0)

    greet("row", in_row, ROWS)
    greet("group", in_block, 8)
    greet("group", in_blocks, 4)

    def push(src, dst, k, device):
        pltpu.make_async_remote_copy(
            src_ref=src, dst_ref=dst, send_sem=send.at[k], recv_sem=recv.at[k],
            device_id=device, device_id_type=MESH,
        ).start()

    def arrived(shape_of, k):
        pltpu.make_async_copy(shape_of, shape_of, recv.at[k]).wait()

    def left(shape_of, k):
        pltpu.make_async_copy(shape_of, shape_of, send.at[k]).wait()

    def push_all(axis, pick, count, src, dst, k):
        def body(d, c):
            t = pick(d)
            push(src(t), dst, k, {axis: t})
            return c

        lax.fori_loop(1, count, body, 0)

    slot_iota = lax.broadcasted_iota(jnp.int32, (S, 64), 0)
    member = [jnp.where(slots_ref[f] == slot_iota, 1.0, 0.0) for f in range(2)]
    member_b = [m.astype(BF16) for m in member]
    count = jnp.sum(member[0] + member[1], axis=1, keepdims=True)
    for a, ref in enumerate((k_ref, v_ref)):
        total = dot(member_b[0], ref[0:64, :]) + dot(member_b[1], ref[64:128, :])
        for s in range(S):
            ms[a * S + s, :, 0:FEATS] = total[s : s + 1]
            ms[a * S + s, :, FEATS:] = jnp.broadcast_to(count[s : s + 1], (1, 128))
    rs[r] = ms[r]

    to_pair = select(128, 128, by_pair)

    def arrange(h, c):
        ln = pl.ds(pl.multiple_of(h * 256, 256), 256)
        wide = pl.ds(pl.multiple_of(HALF + h * 256, 256), 256)
        for a, ref in enumerate((q_ref, k_ref, v_ref, g_ref)):
            cs[:, a, :, ln] = dot(to_pair, ref[:, wide]).astype(BF16).reshape(8, 16, 256)
        return c

    lax.fori_loop(0, 5, arrange, 0)
    mine = pl.ds(pl.multiple_of(hh * PART, 128), PART)
    cr[r] = cs[jp, :, :, mine]

    pl.semaphore_wait(barrier, 15 + 7 + 3)

    push_all("row", in_row, ROWS, lambda t: ms.at[t], rs.at[r], 0)

    before = lax.rem(r + ROWS - 1, ROWS)
    after = lax.rem(r + 1, ROWS)
    rows_half = (slice(None), pl.ds(0, HALF))
    push(k_ref.at[rows_half], hr.at[1, 0], 5, {"row": before})
    push(v_ref.at[rows_half], hr.at[1, 1], 6, {"row": before})
    push(k_ref.at[rows_half], hr.at[0, 0], 7, {"row": after})
    push(v_ref.at[rows_half], hr.at[0, 1], 8, {"row": after})

    def scatter(d, c):
        t = in_row(d)
        tx = t // 4
        ty = t % 4
        tyh = ty // 2
        tjp = tx + tyh * (7 - 2 * tx)
        lanes = pl.ds(pl.multiple_of((ty % 2) * PART, 128), PART)
        push(cs.at[tjp, :, :, lanes], cr.at[r], 4, {"row": t})
        return c

    lax.fori_loop(1, ROWS, scatter, 0)

    log_rate = jnp.log(
        jnp.concatenate([jnp.full((1, 128), decay_ref[h], F32) for h in range(20)], axis=1)
    )

    def power(e, valid):
        return jnp.where(valid, jnp.exp(log_rate * e.astype(F32)), 0.0)

    def combine(rs_, zp_, zb_, bp_, bt_, mp_, mem_, k, forward, norm):
        arrived(rs_.at[pl.ds(0, 15)], k)
        total = jnp.sum(rs_[...], axis=0)
        if norm is None:
            norm = 1.0 / jnp.sqrt(jnp.maximum(total[:, FEATS : FEATS + 1], 1.0))
            piece = total[:, :FEATS] * norm
        else:
            piece = total
        zp_[0] = piece
        zb_[idx] = piece
        push_all("group", in_block, 8, lambda t: zp_.at[0], zb_.at[idx], k + 1)
        arrived(zb_.at[pl.ds(0, 7)], k + 1)
        inside = jnp.zeros((1, FEATS), F32)
        whole = jnp.zeros((1, FEATS), F32)
        for j in range(8):
            got = zb_[j]
            if forward:
                inside = inside + got * power(idx - 1 - j, j < idx)
                whole = whole + got * jnp.exp(log_rate * float(7 - j))
            else:
                inside = inside + got * power(j - idx - 1, j > idx)
                whole = whole + got * jnp.exp(log_rate * float(j))
        bp_[0] = whole
        bt_[blk] = whole
        push_all("group", in_blocks, 4, lambda t: bp_.at[0], bt_.at[blk], k + 2)
        arrived(bt_.at[pl.ds(0, 3)], k + 2)
        for j in range(4):
            if forward:
                inside = inside + bt_[j] * power(8 * (blk - 1 - j) + idx, j < blk)
            else:
                inside = inside + bt_[j] * power(8 * (j - blk - 1) + 7 - idx, j > blk)
        if not forward:
            inside = inside * norm
        mp_[0] = inside
        mem_[r] = inside
        push_all("row", in_row, ROWS, lambda t: mp_.at[0], mem_.at[r], k + 3)
        arrived(mem_.at[pl.ds(0, 15)], k + 3)
        return norm

    norm = combine(rs, zp, zb, bp, bt, mp, mem, 0, True, None)
    zero = jnp.zeros((S, FEATS), F32)
    m2[S:, :] = zero
    for a, to in enumerate((memk, memv)):
        for s in range(S):
            m2[s : s + 1, :] = mem[a * S + s]
        to[...] = m2[...].astype(BF16)
    dm[0] = zero
    dm[1] = zero

    arrived(cr.at[pl.ds(0, 15)], 4)
    to_stripe = select(256, 256, by_stripe)
    for a in (1, 2, 0, 3):
        block = cr[:, a, :, :].reshape(256, PART)
        sep[a] = dot(to_stripe, block).astype(BF16).reshape(2, 128, PART)
    pair_before = holder(lax.rem(jp + 7, 8), hh)
    pair_after = holder(lax.rem(jp + 1, 8), hh)
    push(sep.at[pl.ds(1, 2), 0], hc.at[1], 9, {"row": pair_before})
    push(sep.at[pl.ds(1, 2), 1], hc.at[0], 10, {"row": pair_after})

    for k in (5, 6, 7, 8):
        arrived(hr.at[0, 0], k)
    row_low = jnp.where(r > 0, 0.0, NEG)
    row_high = jnp.where(r < ROWS - 1, 0.0, NEG)

    def row_head(h, c):
        ln = pl.ds(pl.multiple_of(h * E, E), E)
        keys = jnp.concatenate([hr[0, 0, :, ln], k_ref[:, ln], hr[1, 0, :, ln], memk[:, ln]], axis=0)
        vals = jnp.concatenate([hr[0, 1, :, ln], v_ref[:, ln], hr[1, 1, :, ln], memv[:, ln]], axis=0)
        dq, dk, dv = unit(q_ref[:, ln], g_ref[:, ln], keys, vals, row_low, row_high)
        oq_ref[:, ln] = dq.astype(BF16)
        for a, d in enumerate((dk, dv)):
            gs[0, a, :, ln] = d[0:128].astype(BF16)
            own[a, :, ln] = d[128:256]
            gs[1, a, :, ln] = d[256:384].astype(BF16)
            dm[a, :, ln] = d[384:392]
        return c

    lax.fori_loop(0, 10, row_head, 0)
    push(gs.at[0], gr.at[1], 11, {"row": before})
    push(gs.at[1], gr.at[0], 12, {"row": after})

    arrived(hc.at[1], 9)
    arrived(hc.at[0], 10)
    col_low = jnp.where(jp > 0, 0.0, NEG)
    col_high = jnp.where(jp < 7, 0.0, NEG)

    def col_head(h, c):
        ln = pl.ds(pl.multiple_of(h * E, E), E)
        wide = pl.ds(pl.multiple_of(HALF + hh * PART + h * E, E), E)
        mk = memk[:, wide]
        mv = memv[:, wide]
        k0, k1, k2, k3 = hc[0, 0, :, ln], sep[1, 0, :, ln], sep[1, 1, :, ln], hc[1, 0, :, ln]
        v0, v1, v2, v3 = hc[0, 1, :, ln], sep[2, 0, :, ln], sep[2, 1, :, ln], hc[1, 1, :, ln]
        qa, ka, va = unit(
            sep[0, 0, :, ln], sep[3, 0, :, ln],
            jnp.concatenate([k0, k1, k2, mk], axis=0), jnp.concatenate([v0, v1, v2, mv], axis=0),
            col_low, 0.0,
        )
        for a, d in enumerate((ka, va)):
            cgs[0, a, :, ln] = d[0:128].astype(BF16)
            cown[a, :, ln] = d[128:384]
            dm[a, :, wide] = d[384:392]
        sep[0, 0, :, ln] = qa.astype(BF16)
        qb, kb, vb = unit(
            sep[0, 1, :, ln], sep[3, 1, :, ln],
            jnp.concatenate([k1, k2, k3, mk], axis=0), jnp.concatenate([v1, v2, v3, mv], axis=0),
            0.0, col_high,
        )
        for a, d in enumerate((kb, vb)):
            cgs[1, a, :, ln] = d[256:384].astype(BF16)
            cown[a, :, ln] = cown[a, :, ln] + d[0:256]
            dm[a, :, wide] = dm[a, :, wide] + d[384:392]
        sep[0, 1, :, ln] = qb.astype(BF16)
        return c

    lax.fori_loop(0, 5, col_head, 0)

    for a in range(2):
        for s in range(S):
            ms2[a * S + s] = dm[a, s : s + 1, :]
    rs2[r] = ms2[r]
    push_all("row", in_row, ROWS, lambda t: ms2.at[t], rs2.at[r], 15)
    push(cgs.at[0], cgr.at[1], 13, {"row": pair_before})
    push(cgs.at[1], cgr.at[0], 14, {"row": pair_after})

    from_stripe = select_back(256, 256, by_stripe)
    bsq[...] = dot(from_stripe, sep[0].reshape(256, PART)).astype(BF16).reshape(16, 16, PART)
    brq[jp, :, mine] = bsq[r]
    push_all("row", in_row, ROWS, lambda t: bsq.at[t], brq.at[jp, :, mine], 19)

    arrived(cgr.at[1], 13)
    arrived(cgr.at[0], 14)
    for a in range(2):
        full = jnp.concatenate(
            [
                cown[a, 0:128, :] + cgr[0, a].astype(F32),
                cown[a, 128:256, :] + cgr[1, a].astype(F32),
            ],
            axis=0,
        ).astype(BF16)
        bskv[:, a, :, :] = dot(from_stripe, full).astype(BF16).reshape(16, 16, PART)
    brkv[jp, :, :, mine] = bskv[r]
    push_all("row", in_row, ROWS, lambda t: bskv.at[t], brkv.at[jp, :, :, mine], 20)

    combine(rs2, zp2, zb2, bp2, bt2, mp2, mem2, 15, False, norm)
    for a in range(2):
        for s in range(S):
            dm[a, s : s + 1, :] = mem2[a * S + s]

    arrived(gr.at[1], 11)
    arrived(gr.at[0], 12)
    arrived(bsq.at[pl.ds(0, 15)], 19)
    arrived(bskv.at[pl.ds(0, 15)], 20)
    from_pair = select_back(128, 128, by_pair)

    def finish(h, c):
        ln = pl.ds(pl.multiple_of(h * E, E), E)
        wide = pl.ds(pl.multiple_of(HALF + h * E, E), E)
        oq_ref[:, wide] = dot(from_pair, brq[:, :, ln].reshape(128, E)).astype(BF16)
        for a, out in enumerate((ok_ref, ov_ref)):
            back = dot(from_pair, brkv[:, a, :, ln].reshape(128, E))
            dr = dm[a, :, ln].astype(BF16)
            dc = dm[a, :, wide].astype(BF16)
            add_r = jnp.concatenate([dot(member_b[f], dr, 0, 0) for f in range(2)], axis=0)
            add_c = jnp.concatenate([dot(member_b[f], dc, 0, 0) for f in range(2)], axis=0)
            near = gr[0, a, :, ln].astype(F32) + gr[1, a, :, ln].astype(F32)
            out[:, ln] = (own[a, :, ln] + near + add_r).astype(BF16)
            out[:, wide] = (back + add_c).astype(BF16)
        return c

    lax.fori_loop(0, 10, finish, 0)

    left(ms.at[pl.ds(0, 15)], 0)
    left(zb.at[pl.ds(0, 7)], 1)
    left(bt.at[pl.ds(0, 3)], 2)
    left(mem.at[pl.ds(0, 15)], 3)
    left(cr.at[pl.ds(0, 15)], 4)
    for k in (5, 6, 7, 8):
        left(hr.at[0, 0], k)
    left(hc.at[1], 9)
    left(hc.at[0], 10)
    left(gs.at[0], 11)
    left(gs.at[1], 12)
    left(cgs.at[0], 13)
    left(cgs.at[1], 14)
    left(ms2.at[pl.ds(0, 15)], 15)
    left(zb2.at[pl.ds(0, 7)], 16)
    left(bt2.at[pl.ds(0, 3)], 17)
    left(mem2.at[pl.ds(0, 15)], 18)
    left(bsq.at[pl.ds(0, 15)], 19)
    left(bskv.at[pl.ds(0, 15)], 20)


def per_device(queries, keys, values, out_grad, slots, decay):
    flat = (TOKENS, FEATS)
    vm = pl.BlockSpec(memory_space=pltpu.VMEM)

    def row(count, width=FEATS):
        return pltpu.VMEM((count, 1, width), F32)

    scratch = [
        row(16, FEATS + 128), row(16, FEATS + 128),
        row(1), row(8), row(1), row(4), row(1), row(16),
        pltpu.VMEM((16, FEATS), BF16), pltpu.VMEM((16, FEATS), BF16),
        row(16), row(16),
        row(1), row(8), row(1), row(4), row(1), row(16),
        pltpu.VMEM((16, FEATS), F32), pltpu.VMEM((2, S, FEATS), F32),
        pltpu.VMEM((8, 4, 16, HALF), BF16),
        pltpu.VMEM((16, 4, 16, PART), BF16),
        pltpu.VMEM((4, 2, 128, PART), BF16),
        pltpu.VMEM((2, 2, 128, HALF), BF16),
        pltpu.VMEM((2, 2, 128, PART), BF16),
        pltpu.VMEM((2, 2, 128, HALF), BF16),
        pltpu.VMEM((2, 2, 128, HALF), BF16),
        pltpu.VMEM((2, 128, HALF), F32),
        pltpu.VMEM((2, 256, PART), F32),
        pltpu.VMEM((2, 2, 128, PART), BF16),
        pltpu.VMEM((2, 2, 128, PART), BF16),
        pltpu.VMEM((16, 16, PART), BF16),
        pltpu.VMEM((16, 2, 16, PART), BF16),
        pltpu.VMEM((8, 16, HALF), BF16),
        pltpu.VMEM((8, 2, 16, HALF), BF16),
        pltpu.SemaphoreType.DMA((21,)),
        pltpu.SemaphoreType.DMA((21,)),
    ]
    outs = pl.pallas_call(
        kernel,
        out_shape=[jax.ShapeDtypeStruct(flat, BF16)] * 3,
        in_specs=[vm] * 5 + [pl.BlockSpec(memory_space=pltpu.SMEM)],
        out_specs=[vm] * 3,
        scratch_shapes=scratch,
        compiler_params=pltpu.CompilerParams(
            collective_id=0, has_side_effects=True, vmem_limit_bytes=48 * 1024 * 1024
        ),
    )(
        queries.reshape(flat), keys.reshape(flat), values.reshape(flat), out_grad.reshape(flat),
        slots, decay,
    )
    return tuple(o.reshape(queries.shape) for o in outs)


def solution(mesh):
    spec = P("group", "row", None, None)
    return jax.shard_map(
        per_device,
        mesh=mesh,
        in_specs=(spec, spec, spec, spec, P("group", "row", None), P()),
        out_specs=(spec, spec, spec),
        check_vma=False,
    )
```

time: 958 us -> 133 us (0.14)
  the two profiles are of different devices: /device:TPU:101 before, /device:TPU:1 now
where the time goes in v1:
time: 133 us; the launch traced here: 131 us
  Pallas kernels  123 us (92%)
  local copies, waits for them, and re-layouts  7.52 us (6%)
    pallas_call x1, Pallas kernels, per_device(): pl.pallas_call(kernel, out_shape=[jax.ShapeDtypeStruct(flat, BF16)] * 3,...  123 us
    unnamed x15, local copies, waits for them, and re-layouts  7.52 us

profile of v1, /device:TPU:1, one launch (start us, length us, event | category | flops | bytes accessed | tf_op | source)
XLA Modules:
  0.0 131.0 jit_solution(11707290995753201924)
XLA Ops:
  0.6 0.0 copy-start.4
  0.6 0.0 copy-start.5
  0.7 0.7 copy-done.4
  1.3 0.0 copy-done.5
  1.3 0.0 copy-start
  1.3 1.1 copy-done
  2.4 0.0 copy-start.1
  2.4 1.1 copy-done.1
  3.5 0.0 copy-start.2
  3.5 1.1 copy-done.2
  4.6 0.0 copy-start.3
  4.6 1.1 copy-done.3
  5.7 122.8 %shard_map.85 = (bf16[128,2560]{1,0:T(8,128)(2,1)S(1)}, bf16[128,2560]{1,0:T(8,128)(2,1)S(1)}, bf16[128,2560]{1,0:T(8,128)(2,1)S(1)}) custom-call(bf16[128,2560]{1,0:T(8,128)(2,1)S(1)} %bitcast.16, bf16[128,2560]{1,0:T(8,128)(2,1)S(1)} %bitcast.17, bf16[128,2560]{1,0:T(8,128)(2,1)S(1)} %bitcast.18, bf16[128,2560]{1,0:T(8,128)(2,1)S(1)} %bitcast.19, ...), custom_call_target="tpu_custom_call" | custom-call | tf_op jit(solution)/shard_map/pallas_call | solution.py:412
  128.5 0.8 copy.15
  129.3 0.8 copy.16
  130.1 0.8 copy.17
Async XLA Ops:
  0.6 0.7 copy-start.4
  0.6 0.7 copy-start.5
  1.3 1.1 copy-start
  2.4 1.1 copy-start.1
  3.5 1.1 copy-start.2
  4.6 1.1 copy-start.3

commit v2 on v1

v2 whole, which is shorter than its diff:
```python
import jax
import jax.numpy as jnp
from jax import lax
from jax.experimental import pallas as pl
from jax.experimental.pallas import tpu as pltpu
from jax.sharding import PartitionSpec as P

S = 8
E = 128
TOKENS = 128
HALF = 1280
PART = 640
FEATS = 2560
ROWS = 16
MESH = pl.DeviceIdType.MESH
F32 = jnp.float32
BF16 = jnp.bfloat16
NEG = -1e30


def select(rows, cols, source):
    o = lax.broadcasted_iota(jnp.int32, (rows, cols), 0)
    i = lax.broadcasted_iota(jnp.int32, (rows, cols), 1)
    return jnp.where(source(o) == i, 1.0, 0.0).astype(BF16)


def select_back(rows, cols, source):
    i = lax.broadcasted_iota(jnp.int32, (rows, cols), 0)
    o = lax.broadcasted_iota(jnp.int32, (rows, cols), 1)
    return jnp.where(source(o) == i, 1.0, 0.0).astype(BF16)


def by_pair(s):
    return ((s >> 3) & 1) * 64 + (s >> 4) * 8 + (s & 7)


def by_stripe(o):
    return ((o >> 3) & 15) * 16 + ((o >> 2) & 1) * 8 + (o >> 7) * 4 + (o & 3)


def dot(a, b, ca=1, cb=0):
    return lax.dot_general(a, b, (((ca,), (cb,)), ((), ())), preferred_element_type=F32)


def unit(q, g, keys, values, low, high):
    scale = E ** (-0.5)
    s = dot(keys, q, 1, 1) * scale
    used = lax.broadcasted_iota(jnp.int32, (16, 128), 0) < S
    s = jnp.concatenate(
        [s[:128] + low, s[128:256], s[256:384] + high, jnp.where(used, s[384:], NEG)], axis=0
    )
    top = jnp.max(s, axis=0, keepdims=True)
    w = jnp.exp(s - top)
    p = w * (1.0 / jnp.sum(w, axis=0, keepdims=True))
    pb = p.astype(BF16)
    dprob = dot(values, g, 1, 1)
    delta = jnp.sum(pb.astype(F32) * dprob, axis=0, keepdims=True)
    ds = (p * ((dprob - delta) * scale)).astype(BF16)
    dk = dot(ds, q)
    dv = dot(pb, g)
    dq = dot(ds, keys, 0, 0)
    return dq, dk, dv


def kernel(
    qh_ref, kh_ref, vh_ref, gh_ref, slots_ref, decay_ref,
    oq_ref, ok_ref, ov_ref,
    q_ref, k_ref, v_ref, g_ref, wts,
    ms, rs, zp, zb, bp, bt, mp, mem, memk, memv,
    ms2, rs2, zp2, zb2, bp2, bt2, mp2, mem2,
    m2, dm,
    cskv, csqg, crkv, crqg, sep, hr, hc, gs, gr, own, cown, cgs, cgr,
    bsq, bskv, brq, brkv,
    send, recv, load,
):
    r = lax.axis_index("row")
    n = lax.axis_index("group")
    blk = n // 8
    idx = n % 8
    x = r // 4
    y = r % 4
    hh = y % 2
    yh = y // 2
    jp = x + yh * (7 - 2 * x)

    def holder(pair, part):
        high = pair // 4
        low = pair % 4
        return (low + high * (3 - 2 * low)) * 4 + high * 2 + part

    def in_row(d):
        return lax.rem(r + d, ROWS)

    def in_block(d):
        return blk * 8 + lax.rem(idx + d, 8)

    def in_blocks(d):
        return lax.rem(blk + d, 4) * 8 + idx

    barrier = pltpu.get_barrier_semaphore()

    def greet(axis, pick, count):
        def body(d, c):
            pl.semaphore_signal(barrier, inc=1, device_id={axis: pick(d)}, device_id_type=MESH)
            return c

        lax.fori_loop(1, count, body, 0)

    greet("row", in_row, ROWS)
    greet("group", in_block, 8)
    greet("group", in_blocks, 4)

    pairs = ((kh_ref, k_ref), (vh_ref, v_ref), (qh_ref, q_ref), (gh_ref, g_ref))

    def fetch(a, part):
        cols = (slice(None), pl.ds(part * HALF, HALF))
        return pltpu.make_async_copy(
            pairs[a][0].at[cols], pairs[a][1].at[cols], load.at[a * 2 + part]
        )

    for part in (1, 0):
        for a in range(4):
            fetch(a, part).start()

    def push(src, dst, k, device):
        pltpu.make_async_remote_copy(
            src_ref=src, dst_ref=dst, send_sem=send.at[k], recv_sem=recv.at[k],
            device_id=device, device_id_type=MESH,
        ).start()

    def arrived(shape_of, k):
        pltpu.make_async_copy(shape_of, shape_of, recv.at[k]).wait()

    def left(shape_of, k):
        pltpu.make_async_copy(shape_of, shape_of, send.at[k]).wait()

    def push_all(axis, pick, count, src, dst, k):
        def body(d, c):
            t = pick(d)
            push(src(t), dst, k, {axis: t})
            return c

        lax.fori_loop(1, count, body, 0)

    to_pair = select(128, 128, by_pair)
    mine = pl.ds(pl.multiple_of(hh * PART, 128), PART)

    def arrange(first, second, to):
        def body(h, c):
            ln = pl.ds(pl.multiple_of(h * 256, 256), 256)
            wide = pl.ds(pl.multiple_of(HALF + h * 256, 256), 256)
            for a, ref in enumerate((first, second)):
                to[:, a, :, ln] = dot(to_pair, ref[:, wide]).astype(BF16).reshape(8, 16, 256)
            return c

        lax.fori_loop(0, 5, body, 0)

    fetch(0, 1).wait()
    fetch(1, 1).wait()
    arrange(k_ref, v_ref, cskv)
    crkv[r] = cskv[jp, :, :, mine]
    fetch(2, 1).wait()
    fetch(3, 1).wait()
    arrange(q_ref, g_ref, csqg)
    crqg[r] = csqg[jp, :, :, mine]

    fetch(0, 0).wait()
    fetch(1, 0).wait()
    slot_iota = lax.broadcasted_iota(jnp.int32, (S, 64), 0)
    member = [jnp.where(slots_ref[f] == slot_iota, 1.0, 0.0) for f in range(2)]
    member_b = [m.astype(BF16) for m in member]
    count = jnp.sum(member[0] + member[1], axis=1, keepdims=True)
    for a, ref in enumerate((k_ref, v_ref)):
        total = dot(member_b[0], ref[0:64, :]) + dot(member_b[1], ref[64:128, :])
        for s in range(S):
            ms[a * S + s, :, 0:FEATS] = total[s : s + 1]
            ms[a * S + s, :, FEATS:] = jnp.broadcast_to(count[s : s + 1], (1, 128))
    rs[r] = ms[r]

    log_rate = jnp.log(
        jnp.concatenate([jnp.full((1, 128), decay_ref[h], F32) for h in range(20)], axis=1)
    )

    def power(e):
        return jnp.exp(log_rate * e.astype(F32))

    for j in range(8):
        wts[j] = jnp.where(j < idx, power(idx - 1 - j), 0.0)
        wts[8 + j] = jnp.exp(log_rate * float(7 - j))
        wts[20 + j] = jnp.where(j > idx, power(j - idx - 1), 0.0)
        wts[28 + j] = jnp.exp(log_rate * float(j))
    for j in range(4):
        wts[16 + j] = jnp.where(j < blk, power(8 * (blk - 1 - j) + idx), 0.0)
        wts[36 + j] = jnp.where(j > blk, power(8 * (j - blk - 1) + 7 - idx), 0.0)

    fetch(2, 0).wait()
    fetch(3, 0).wait()
    pl.semaphore_wait(barrier, 15 + 7 + 3)

    def scatter(source, to, k):
        def body(d, c):
            t = in_row(d)
            tx = t // 4
            ty = t % 4
            tyh = ty // 2
            tjp = tx + tyh * (7 - 2 * tx)
            lanes = pl.ds(pl.multiple_of((ty % 2) * PART, 128), PART)
            push(source.at[tjp, :, :, lanes], to.at[r], k, {"row": t})
            return c

        lax.fori_loop(1, ROWS, body, 0)

    push_all("row", in_row, ROWS, lambda t: ms.at[t], rs.at[r], 0)
    scatter(cskv, crkv, 4)
    scatter(csqg, crqg, 21)

    def to_the_block(piece, zp_, zb_, k):
        zp_[0] = piece
        zb_[idx] = piece
        push_all("group", in_block, 8, lambda t: zp_.at[0], zb_.at[idx], k)

    def to_the_blocks(zb_, bp_, bt_, k, first):
        arrived(zb_.at[pl.ds(0, 7)], k - 1)
        whole = jnp.sum(zb_[...] * wts[first + 8 : first + 16], axis=0)
        bp_[0] = whole
        bt_[blk] = whole
        push_all("group", in_blocks, 4, lambda t: bp_.at[0], bt_.at[blk], k)
        return jnp.sum(zb_[...] * wts[first : first + 8], axis=0)

    def to_the_row(inside, bt_, mp_, mem_, k, first, norm_):
        arrived(bt_.at[pl.ds(0, 3)], k - 1)
        inside = inside + jnp.sum(bt_[...] * wts[first + 16 : first + 20], axis=0)
        if norm_ is not None:
            inside = inside * norm_
        mp_[0] = inside
        mem_[r] = inside
        push_all("row", in_row, ROWS, lambda t: mp_.at[0], mem_.at[r], k)

    arrived(rs.at[pl.ds(0, 15)], 0)
    total = jnp.sum(rs[...], axis=0)
    norm = 1.0 / jnp.sqrt(jnp.maximum(total[:, FEATS : FEATS + 1], 1.0))
    to_the_block(total[:, :FEATS] * norm, zp, zb, 1)

    to_stripe = select(256, 256, by_stripe)

    def split(from_, a, to):
        block = from_[:, a, :, :].reshape(256, PART)
        sep[to] = dot(to_stripe, block).astype(BF16).reshape(2, 128, PART)

    pair_before = holder(lax.rem(jp + 7, 8), hh)
    pair_after = holder(lax.rem(jp + 1, 8), hh)
    arrived(crkv.at[pl.ds(0, 15)], 4)
    split(crkv, 0, 1)
    split(crkv, 1, 2)
    push(sep.at[pl.ds(1, 2), 0], hc.at[1], 9, {"row": pair_before})
    push(sep.at[pl.ds(1, 2), 1], hc.at[0], 10, {"row": pair_after})

    inside = to_the_blocks(zb, bp, bt, 2, 0)
    to_the_row(inside, bt, mp, mem, 3, 0, None)

    arrived(crqg.at[pl.ds(0, 15)], 21)
    before = lax.rem(r + ROWS - 1, ROWS)
    after = lax.rem(r + 1, ROWS)
    rows_half = (slice(None), pl.ds(0, HALF))
    push(k_ref.at[rows_half], hr.at[1, 0], 5, {"row": before})
    push(k_ref.at[rows_half], hr.at[0, 0], 7, {"row": after})
    push(v_ref.at[rows_half], hr.at[1, 1], 6, {"row": before})
    push(v_ref.at[rows_half], hr.at[0, 1], 8, {"row": after})
    split(crqg, 0, 0)
    split(crqg, 1, 3)

    arrived(mem.at[pl.ds(0, 15)], 3)
    zero = jnp.zeros((S, FEATS), F32)
    m2[S:, :] = zero
    for a, to in enumerate((memk, memv)):
        for s in range(S):
            m2[s : s + 1, :] = mem[a * S + s]
        to[...] = m2[...].astype(BF16)
    dm[0] = zero
    dm[1] = zero

    arrived(hc.at[1], 9)
    arrived(hc.at[0], 10)
    col_low = jnp.where(jp > 0, 0.0, NEG)
    col_high = jnp.where(jp < 7, 0.0, NEG)

    def col_head(h, c):
        ln = pl.ds(pl.multiple_of(h * E, E), E)
        wide = pl.ds(pl.multiple_of(HALF + hh * PART + h * E, E), E)
        mk = memk[:, wide]
        mv = memv[:, wide]
        k0, k1, k2, k3 = hc[0, 0, :, ln], sep[1, 0, :, ln], sep[1, 1, :, ln], hc[1, 0, :, ln]
        v0, v1, v2, v3 = hc[0, 1, :, ln], sep[2, 0, :, ln], sep[2, 1, :, ln], hc[1, 1, :, ln]
        qa, ka, va = unit(
            sep[0, 0, :, ln], sep[3, 0, :, ln],
            jnp.concatenate([k0, k1, k2, mk], axis=0), jnp.concatenate([v0, v1, v2, mv], axis=0),
            col_low, 0.0,
        )
        qb, kb, vb = unit(
            sep[0, 1, :, ln], sep[3, 1, :, ln],
            jnp.concatenate([k1, k2, k3, mk], axis=0), jnp.concatenate([v1, v2, v3, mv], axis=0),
            0.0, col_high,
        )
        for a, (da, db) in enumerate(((ka, kb), (va, vb))):
            cgs[0, a, :, ln] = da[0:128].astype(BF16)
            cown[a, :, ln] = da[128:384] + db[0:256]
            cgs[1, a, :, ln] = db[256:384].astype(BF16)
            dm[a, :, wide] = da[384:392] + db[384:392]
        sep[0, 0, :, ln] = qa.astype(BF16)
        sep[0, 1, :, ln] = qb.astype(BF16)
        return c

    lax.fori_loop(0, 5, col_head, 0)
    push(cgs.at[0], cgr.at[1], 13, {"row": pair_before})
    push(cgs.at[1], cgr.at[0], 14, {"row": pair_after})
    from_stripe = select_back(256, 256, by_stripe)
    bsq[...] = dot(from_stripe, sep[0].reshape(256, PART)).astype(BF16).reshape(16, 16, PART)
    brq[jp, :, mine] = bsq[r]
    push_all("row", in_row, ROWS, lambda t: bsq.at[t], brq.at[jp, :, mine], 19)

    for k in (5, 7, 6, 8):
        arrived(hr.at[0, 0], k)
    row_low = jnp.where(r > 0, 0.0, NEG)
    row_high = jnp.where(r < ROWS - 1, 0.0, NEG)

    def row_head(h, c):
        ln = pl.ds(pl.multiple_of(h * E, E), E)
        keys = jnp.concatenate([hr[0, 0, :, ln], k_ref[:, ln], hr[1, 0, :, ln], memk[:, ln]], axis=0)
        vals = jnp.concatenate([hr[0, 1, :, ln], v_ref[:, ln], hr[1, 1, :, ln], memv[:, ln]], axis=0)
        dq, dk, dv = unit(q_ref[:, ln], g_ref[:, ln], keys, vals, row_low, row_high)
        oq_ref[:, ln] = dq.astype(BF16)
        for a, d in enumerate((dk, dv)):
            gs[0, a, :, ln] = d[0:128].astype(BF16)
            own[a, :, ln] = d[128:256]
            gs[1, a, :, ln] = d[256:384].astype(BF16)
            dm[a, :, ln] = d[384:392]
        return c

    lax.fori_loop(0, 10, row_head, 0)

    for a in range(2):
        for s in range(S):
            ms2[a * S + s] = dm[a, s : s + 1, :]
    rs2[r] = ms2[r]
    push_all("row", in_row, ROWS, lambda t: ms2.at[t], rs2.at[r], 15)
    push(gs.at[0], gr.at[1], 11, {"row": before})
    push(gs.at[1], gr.at[0], 12, {"row": after})

    arrived(cgr.at[1], 13)
    arrived(cgr.at[0], 14)
    for a in range(2):
        full = jnp.concatenate(
            [
                cown[a, 0:128, :] + cgr[0, a].astype(F32),
                cown[a, 128:256, :] + cgr[1, a].astype(F32),
            ],
            axis=0,
        ).astype(BF16)
        bskv[:, a, :, :] = dot(from_stripe, full).astype(BF16).reshape(16, 16, PART)
    brkv[jp, :, :, mine] = bskv[r]
    push_all("row", in_row, ROWS, lambda t: bskv.at[t], brkv.at[jp, :, :, mine], 20)

    arrived(rs2.at[pl.ds(0, 15)], 15)
    to_the_block(jnp.sum(rs2[...], axis=0), zp2, zb2, 16)
    inside = to_the_blocks(zb2, bp2, bt2, 17, 20)
    to_the_row(inside, bt2, mp2, mem2, 18, 20, norm)

    from_pair = select_back(128, 128, by_pair)
    arrived(bsq.at[pl.ds(0, 15)], 19)

    def finish_q(h, c):
        ln = pl.ds(pl.multiple_of(h * 256, 256), 256)
        wide = pl.ds(pl.multiple_of(HALF + h * 256, 256), 256)
        oq_ref[:, wide] = dot(from_pair, brq[:, :, ln].reshape(128, 256)).astype(BF16)
        return c

    lax.fori_loop(0, 5, finish_q, 0)
    arrived(mem2.at[pl.ds(0, 15)], 18)
    for a in range(2):
        for s in range(S):
            dm[a, s : s + 1, :] = mem2[a * S + s]
    arrived(gr.at[1], 11)
    arrived(gr.at[0], 12)
    arrived(bskv.at[pl.ds(0, 15)], 20)

    def finish(h, c):
        ln = pl.ds(pl.multiple_of(h * 256, 256), 256)
        wide = pl.ds(pl.multiple_of(HALF + h * 256, 256), 256)
        for a, out in enumerate((ok_ref, ov_ref)):
            back = dot(from_pair, brkv[:, a, :, ln].reshape(128, 256))
            dr = dm[a, :, ln].astype(BF16)
            dc = dm[a, :, wide].astype(BF16)
            add_r = jnp.concatenate([dot(member_b[f], dr, 0, 0) for f in range(2)], axis=0)
            add_c = jnp.concatenate([dot(member_b[f], dc, 0, 0) for f in range(2)], axis=0)
            near = gr[0, a, :, ln].astype(F32) + gr[1, a, :, ln].astype(F32)
            out[:, ln] = (own[a, :, ln] + near + add_r).astype(BF16)
            out[:, wide] = (back + add_c).astype(BF16)
        return c

    lax.fori_loop(0, 5, finish, 0)

    left(ms.at[pl.ds(0, 15)], 0)
    left(zb.at[pl.ds(0, 7)], 1)
    left(bt.at[pl.ds(0, 3)], 2)
    left(mem.at[pl.ds(0, 15)], 3)
    left(crkv.at[pl.ds(0, 15)], 4)
    left(crqg.at[pl.ds(0, 15)], 21)
    for k in (5, 6, 7, 8):
        left(hr.at[0, 0], k)
    left(hc.at[1], 9)
    left(hc.at[0], 10)
    left(gs.at[0], 11)
    left(gs.at[1], 12)
    left(cgs.at[0], 13)
    left(cgs.at[1], 14)
    left(ms2.at[pl.ds(0, 15)], 15)
    left(zb2.at[pl.ds(0, 7)], 16)
    left(bt2.at[pl.ds(0, 3)], 17)
    left(mem2.at[pl.ds(0, 15)], 18)
    left(bsq.at[pl.ds(0, 15)], 19)
    left(bskv.at[pl.ds(0, 15)], 20)


def per_device(queries, keys, values, out_grad, slots, decay):
    flat = (TOKENS, FEATS)
    vm = pl.BlockSpec(memory_space=pltpu.VMEM)

    def row(count, width=FEATS):
        return pltpu.VMEM((count, 1, width), F32)

    scratch = [
        *[pltpu.VMEM(flat, BF16)] * 4, row(40),
        row(16, FEATS + 128), row(16, FEATS + 128),
        row(1), row(8), row(1), row(4), row(1), row(16),
        pltpu.VMEM((16, FEATS), BF16), pltpu.VMEM((16, FEATS), BF16),
        row(16), row(16),
        row(1), row(8), row(1), row(4), row(1), row(16),
        pltpu.VMEM((16, FEATS), F32), pltpu.VMEM((2, S, FEATS), F32),
        pltpu.VMEM((8, 2, 16, HALF), BF16),
        pltpu.VMEM((8, 2, 16, HALF), BF16),
        pltpu.VMEM((16, 2, 16, PART), BF16),
        pltpu.VMEM((16, 2, 16, PART), BF16),
        pltpu.VMEM((4, 2, 128, PART), BF16),
        pltpu.VMEM((2, 2, 128, HALF), BF16),
        pltpu.VMEM((2, 2, 128, PART), BF16),
        pltpu.VMEM((2, 2, 128, HALF), BF16),
        pltpu.VMEM((2, 2, 128, HALF), BF16),
        pltpu.VMEM((2, 128, HALF), F32),
        pltpu.VMEM((2, 256, PART), F32),
        pltpu.VMEM((2, 2, 128, PART), BF16),
        pltpu.VMEM((2, 2, 128, PART), BF16),
        pltpu.VMEM((16, 16, PART), BF16),
        pltpu.VMEM((16, 2, 16, PART), BF16),
        pltpu.VMEM((8, 16, HALF), BF16),
        pltpu.VMEM((8, 2, 16, HALF), BF16),
        pltpu.SemaphoreType.DMA((22,)),
        pltpu.SemaphoreType.DMA((22,)),
        pltpu.SemaphoreType.DMA((8,)),
    ]
    outs = pl.pallas_call(
        kernel,
        out_shape=[jax.ShapeDtypeStruct(flat, BF16)] * 3,
        in_specs=[pl.BlockSpec(memory_space=pltpu.HBM)] * 4 + [vm] + [pl.BlockSpec(memory_space=pltpu.SMEM)],
        out_specs=[vm] * 3,
        scratch_shapes=scratch,
        compiler_params=pltpu.CompilerParams(
            collective_id=0, has_side_effects=True, vmem_limit_bytes=48 * 1024 * 1024
        ),
    )(
        *[
            pltpu.with_memory_space_constraint(a.reshape(flat), pltpu.HBM)
            for a in (queries, keys, values, out_grad)
        ],
        slots, decay,
    )
    return tuple(o.reshape(queries.shape) for o in outs)


def solution(mesh):
    spec = P("group", "row", None, None)
    return jax.shard_map(
        per_device,
        mesh=mesh,
        in_specs=(spec, spec, spec, spec, P("group", "row", None), P()),
        out_specs=(spec, spec, spec),
        check_vma=False,
    )
```

time: 133 us -> 115 us (0.86); the launches traced: 131 us -> 115 us
  Pallas kernels: 123 us -> 111 us
  local copies, waits for them, and re-layouts: 7.52 us -> 3.18 us
    pallas_call x1, Pallas kernels: 123 us -> 111 us  [per_device(): pl.pallas_call(kernel, out_shape=[jax.ShapeDtypeStruct(flat, BF16)] * 3,...]
    unnamed x15 -> x7, local copies, waits for them, and re-layouts: 7.52 us -> 3.18 us
where the time goes in v2:
time: 115 us
  Pallas kernels  111 us (97%)
  local copies, waits for them, and re-layouts  3.18 us (3%)
    pallas_call x1, Pallas kernels, per_device(): pl.pallas_call(kernel, out_shape=[jax.ShapeDtypeStruct(flat, BF16)] * 3,...  111 us
    unnamed x7, local copies, waits for them, and re-layouts  3.18 us

profile of v2, /device:TPU:1, one launch (start us, length us, event | category | flops | bytes accessed | tf_op | source)
XLA Modules:
  0.0 115.3 jit_solution(1019604701574602445)
XLA Ops:
  0.6 0.0 copy-start
  0.6 0.0 copy-start.1
  0.7 0.7 copy-done
  1.3 0.0 copy-done.1
  1.3 111.5 %shard_map.85 = (bf16[128,2560]{1,0:T(8,128)(2,1)S(1)}, bf16[128,2560]{1,0:T(8,128)(2,1)S(1)}, bf16[128,2560]{1,0:T(8,128)(2,1)S(1)}) custom-call(bf16[128,2560]{1,0:T(8,128)(2,1)} %bitcast.16, bf16[128,2560]{1,0:T(8,128)(2,1)} %bitcast.17, bf16[128,2560]{1,0:T(8,128)(2,1)} %bitcast.18, bf16[128,2560]{1,0:T(8,128)(2,1)} %bitcast.19, ...), custom_call_target="tpu_custom_call" | custom-call | tf_op jit(solution)/shard_map/pallas_call | solution.py:460
  112.8 0.8 copy.15
  113.6 0.8 copy.16
  114.5 0.8 copy.17
Async XLA Ops:
  0.6 0.7 copy-start
  0.6 0.7 copy-start.1

commit v3 on v2

--- a/solution.py
+++ b/solution.py
@@ -16,6 +16,12 @@
 F32 = jnp.float32
 BF16 = jnp.bfloat16
 NEG = -1e30
+STEPS = (
+    (1, 0), (0, 1), (3, 0), (0, 3), (1, 1), (3, 3), (1, 3), (3, 1),
+    (2, 0), (0, 2), (2, 1), (1, 2), (2, 3), (3, 2), (2, 2),
+)
+STEPS_X = sum(dx * 4**i for i, (dx, _) in enumerate(STEPS))
+STEPS_Y = sum(dy * 4**i for i, (_, dy) in enumerate(STEPS))
 
 
 def select(rows, cols, source):
@@ -79,17 +85,25 @@
     idx = n % 8
     x = r // 4
     y = r % 4
-    hh = y % 2
-    yh = y // 2
+    hh = y // 2
+    yh = y % 2
     jp = x + yh * (7 - 2 * x)
 
     def holder(pair, part):
         high = pair // 4
         low = pair % 4
-        return (low + high * (3 - 2 * low)) * 4 + high * 2 + part
+        return (low + high * (3 - 2 * low)) * 4 + part * 2 + high
 
     def in_row(d):
         return lax.rem(r + d, ROWS)
+
+    def around(visit):
+        def body(d, c):
+            dx, dy = c
+            visit(lax.rem(x + dx % 4, 4), lax.rem(y + dy % 4, 4))
+            return dx // 4, dy // 4
+
+        lax.fori_loop(0, len(STEPS), body, (jnp.int32(STEPS_X), jnp.int32(STEPS_Y)))
 
     def in_block(d):
         return blk * 8 + lax.rem(idx + d, 8)
@@ -118,8 +132,8 @@
             pairs[a][0].at[cols], pairs[a][1].at[cols], load.at[a * 2 + part]
         )
 
-    for part in (1, 0):
-        for a in range(4):
+    for a in range(4):
+        for part in (1, 0):
             fetch(a, part).start()
 
     def push(src, dst, k, device):
@@ -141,6 +155,13 @@
             return c
 
         lax.fori_loop(1, count, body, 0)
+
+    def push_row(src, dst, k):
+        def visit(tx, ty):
+            t = tx * 4 + ty
+            push(src(t), dst, k, {"row": t})
+
+        around(visit)
 
     to_pair = select(128, 128, by_pair)
     mine = pl.ds(pl.multiple_of(hh * PART, 128), PART)
@@ -155,17 +176,9 @@
 
         lax.fori_loop(0, 5, body, 0)
 
-    fetch(0, 1).wait()
-    fetch(1, 1).wait()
-    arrange(k_ref, v_ref, cskv)
-    crkv[r] = cskv[jp, :, :, mine]
-    fetch(2, 1).wait()
-    fetch(3, 1).wait()
-    arrange(q_ref, g_ref, csqg)
-    crqg[r] = csqg[jp, :, :, mine]
-
-    fetch(0, 0).wait()
-    fetch(1, 0).wait()
+    for part in range(2):
+        for a in range(2):
+            fetch(a, part).wait()
     slot_iota = lax.broadcasted_iota(jnp.int32, (S, 64), 0)
     member = [jnp.where(slots_ref[f] == slot_iota, 1.0, 0.0) for f in range(2)]
     member_b = [m.astype(BF16) for m in member]
@@ -177,6 +190,26 @@
             ms[a * S + s, :, FEATS:] = jnp.broadcast_to(count[s : s + 1], (1, 128))
     rs[r] = ms[r]
 
+    pl.semaphore_wait(barrier, 15 + 7 + 3)
+    push_row(lambda t: ms.at[t], rs.at[r], 0)
+
+    def scatter(source, to, k):
+        def visit(tx, ty):
+            tjp = tx + (ty % 2) * (7 - 2 * tx)
+            lanes = pl.ds(pl.multiple_of((ty // 2) * PART, 128), PART)
+            push(source.at[tjp, :, :, lanes], to.at[r], k, {"row": tx * 4 + ty})
+
+        around(visit)
+
+    arrange(k_ref, v_ref, cskv)
+    scatter(cskv, crkv, 4)
+    crkv[r] = cskv[jp, :, :, mine]
+    fetch(2, 1).wait()
+    fetch(3, 1).wait()
+    arrange(q_ref, g_ref, csqg)
+    scatter(csqg, crqg, 21)
+    crqg[r] = csqg[jp, :, :, mine]
+
     log_rate = jnp.log(
         jnp.concatenate([jnp.full((1, 128), decay_ref[h], F32) for h in range(20)], axis=1)
     )
@@ -195,24 +228,6 @@
 
     fetch(2, 0).wait()
     fetch(3, 0).wait()
-    pl.semaphore_wait(barrier, 15 + 7 + 3)
-
-    def scatter(source, to, k):
-        def body(d, c):
-            t = in_row(d)
-            tx = t // 4
-            ty = t % 4
-            tyh = ty // 2
-            tjp = tx + tyh * (7 - 2 * tx)
-            lanes = pl.ds(pl.multiple_of((ty % 2) * PART, 128), PART)
-            push(source.at[tjp, :, :, lanes], to.at[r], k, {"row": t})
-            return c
-
-        lax.fori_loop(1, ROWS, body, 0)
-
-    push_all("row", in_row, ROWS, lambda t: ms.at[t], rs.at[r], 0)
-    scatter(cskv, crkv, 4)
-    scatter(csqg, crqg, 21)
 
     def to_the_block(piece, zp_, zb_, k):
         zp_[0] = piece
@@ -234,7 +249,7 @@
             inside = inside * norm_
         mp_[0] = inside
         mem_[r] = inside
-        push_all("row", in_row, ROWS, lambda t: mp_.at[0], mem_.at[r], k)
+        push_row(lambda t: mp_.at[0], mem_.at[r], k)
 
     arrived(rs.at[pl.ds(0, 15)], 0)
     total = jnp.sum(rs[...], axis=0)
@@ -261,11 +276,11 @@
     arrived(crqg.at[pl.ds(0, 15)], 21)
     before = lax.rem(r + ROWS - 1, ROWS)
     after = lax.rem(r + 1, ROWS)
-    rows_half = (slice(None), pl.ds(0, HALF))
-    push(k_ref.at[rows_half], hr.at[1, 0], 5, {"row": before})
-    push(k_ref.at[rows_half], hr.at[0, 0], 7, {"row": after})
-    push(v_ref.at[rows_half], hr.at[1, 1], 6, {"row": before})
-    push(v_ref.at[rows_half], hr.at[0, 1], 8, {"row": after})
+    for i in range(2):
+        cols = (slice(None), pl.ds(i * PART, PART))
+        for a, ref in enumerate((k_ref, v_ref)):
+            push(ref.at[cols], hr.at[i, 1, a], 22 + 4 * i + 2 * a, {"row": before})
+            push(ref.at[cols], hr.at[i, 0, a], 23 + 4 * i + 2 * a, {"row": after})
     split(crqg, 0, 0)
     split(crqg, 1, 3)
 
@@ -316,35 +331,49 @@
     from_stripe = select_back(256, 256, by_stripe)
     bsq[...] = dot(from_stripe, sep[0].reshape(256, PART)).astype(BF16).reshape(16, 16, PART)
     brq[jp, :, mine] = bsq[r]
-    push_all("row", in_row, ROWS, lambda t: bsq.at[t], brq.at[jp, :, mine], 19)
-
-    for k in (5, 7, 6, 8):
-        arrived(hr.at[0, 0], k)
+    push_row(lambda t: bsq.at[t], brq.at[jp, :, mine], 19)
+
     row_low = jnp.where(r > 0, 0.0, NEG)
     row_high = jnp.where(r < ROWS - 1, 0.0, NEG)
 
-    def row_head(h, c):
-        ln = pl.ds(pl.multiple_of(h * E, E), E)
-        keys = jnp.concatenate([hr[0, 0, :, ln], k_ref[:, ln], hr[1, 0, :, ln], memk[:, ln]], axis=0)
-        vals = jnp.concatenate([hr[0, 1, :, ln], v_ref[:, ln], hr[1, 1, :, ln], memv[:, ln]], axis=0)
-        dq, dk, dv = unit(q_ref[:, ln], g_ref[:, ln], keys, vals, row_low, row_high)
-        oq_ref[:, ln] = dq.astype(BF16)
-        for a, d in enumerate((dk, dv)):
-            gs[0, a, :, ln] = d[0:128].astype(BF16)
-            own[a, :, ln] = d[128:256]
-            gs[1, a, :, ln] = d[256:384].astype(BF16)
-            dm[a, :, ln] = d[384:392]
-        return c
-
-    lax.fori_loop(0, 10, row_head, 0)
+    def row_heads(i):
+        for k in range(4):
+            arrived(hr.at[0, 0, 0], 22 + 4 * i + k)
+
+        def body(h, c):
+            near = pl.ds(pl.multiple_of(h * E, E), E)
+            ln = pl.ds(pl.multiple_of(i * PART + h * E, E), E)
+            keys = jnp.concatenate(
+                [hr[i, 0, 0, :, near], k_ref[:, ln], hr[i, 1, 0, :, near], memk[:, ln]], axis=0
+            )
+            vals = jnp.concatenate(
+                [hr[i, 0, 1, :, near], v_ref[:, ln], hr[i, 1, 1, :, near], memv[:, ln]], axis=0
+            )
+            dq, dk, dv = unit(q_ref[:, ln], g_ref[:, ln], keys, vals, row_low, row_high)
+            oq_ref[:, ln] = dq.astype(BF16)
+            for a, d in enumerate((dk, dv)):
+                gs[i, 0, a, :, near] = d[0:128].astype(BF16)
+                own[a, :, ln] = d[128:256]
+                gs[i, 1, a, :, near] = d[256:384].astype(BF16)
+                dm[a, :, ln] = d[384:392]
+            return c
+
+        lax.fori_loop(0, 5, body, 0)
+
+    def row_back(i):
+        push(gs.at[i, 0], gr.at[i, 1], 5 + 2 * i, {"row": before})
+        push(gs.at[i, 1], gr.at[i, 0], 6 + 2 * i, {"row": after})
+
+    row_heads(0)
+    row_back(0)
+    row_heads(1)
 
     for a in range(2):
         for s in range(S):
             ms2[a * S + s] = dm[a, s : s + 1, :]
     rs2[r] = ms2[r]
-    push_all("row", in_row, ROWS, lambda t: ms2.at[t], rs2.at[r], 15)
-    push(gs.at[0], gr.at[1], 11, {"row": before})
-    push(gs.at[1], gr.at[0], 12, {"row": after})
+    push_row(lambda t: ms2.at[t], rs2.at[r], 15)
+    row_back(1)
 
     arrived(cgr.at[1], 13)
     arrived(cgr.at[0], 14)
@@ -358,7 +387,7 @@
         ).astype(BF16)
         bskv[:, a, :, :] = dot(from_stripe, full).astype(BF16).reshape(16, 16, PART)
     brkv[jp, :, :, mine] = bskv[r]
-    push_all("row", in_row, ROWS, lambda t: bskv.at[t], brkv.at[jp, :, :, mine], 20)
+    push_row(lambda t: bskv.at[t], brkv.at[jp, :, :, mine], 20)
 
     arrived(rs2.at[pl.ds(0, 15)], 15)
     to_the_block(jnp.sum(rs2[...], axis=0), zp2, zb2, 16)
@@ -375,12 +404,18 @@
         return c
 
     lax.fori_loop(0, 5, finish_q, 0)
+    for i in range(2):
+        cols = pl.ds(i * PART, PART)
+        arrived(gr.at[i, 0], 5 + 2 * i)
+        arrived(gr.at[i, 1], 6 + 2 * i)
+        for a in range(2):
+            own[a, :, cols] = (
+                own[a, :, cols] + gr[i, 0, a].astype(F32) + gr[i, 1, a].astype(F32)
+            )
     arrived(mem2.at[pl.ds(0, 15)], 18)
     for a in range(2):
         for s in range(S):
             dm[a, s : s + 1, :] = mem2[a * S + s]
-    arrived(gr.at[1], 11)
-    arrived(gr.at[0], 12)
     arrived(bskv.at[pl.ds(0, 15)], 20)
 
     def finish(h, c):
@@ -392,8 +427,7 @@
             dc = dm[a, :, wide].astype(BF16)
             add_r = jnp.concatenate([dot(member_b[f], dr, 0, 0) for f in range(2)], axis=0)
             add_c = jnp.concatenate([dot(member_b[f], dc, 0, 0) for f in range(2)], axis=0)
-            near = gr[0, a, :, ln].astype(F32) + gr[1, a, :, ln].astype(F32)
-            out[:, ln] = (own[a, :, ln] + near + add_r).astype(BF16)
+            out[:, ln] = (own[a, :, ln] + add_r).astype(BF16)
             out[:, wide] = (back + add_c).astype(BF16)
         return c
 
@@ -405,12 +439,12 @@
     left(mem.at[pl.ds(0, 15)], 3)
     left(crkv.at[pl.ds(0, 15)], 4)
     left(crqg.at[pl.ds(0, 15)], 21)
-    for k in (5, 6, 7, 8):
-        left(hr.at[0, 0], k)
+    for k in range(8):
+        left(hr.at[0, 0, 0], 22 + k)
+    for k in range(4):
+        left(gs.at[0, 0], 5 + k)
     left(hc.at[1], 9)
     left(hc.at[0], 10)
-    left(gs.at[0], 11)
-    left(gs.at[1], 12)
     left(cgs.at[0], 13)
     left(cgs.at[1], 14)
     left(ms2.at[pl.ds(0, 15)], 15)
@@ -441,10 +475,10 @@
         pltpu.VMEM((16, 2, 16, PART), BF16),
         pltpu.VMEM((16, 2, 16, PART), BF16),
         pltpu.VMEM((4, 2, 128, PART), BF16),
-        pltpu.VMEM((2, 2, 128, HALF), BF16),
+        pltpu.VMEM((2, 2, 2, 128, PART), BF16),
         pltpu.VMEM((2, 2, 128, PART), BF16),
-        pltpu.VMEM((2, 2, 128, HALF), BF16),
-        pltpu.VMEM((2, 2, 128, HALF), BF16),
+        pltpu.VMEM((2, 2, 2, 128, PART), BF16),
+        pltpu.VMEM((2, 2, 2, 128, PART), BF16),
         pltpu.VMEM((2, 128, HALF), F32),
         pltpu.VMEM((2, 256, PART), F32),
         pltpu.VMEM((2, 2, 128, PART), BF16),
@@ -453,8 +487,8 @@
         pltpu.VMEM((16, 2, 16, PART), BF16),
         pltpu.VMEM((8, 16, HALF), BF16),
         pltpu.VMEM((8, 2, 16, HALF), BF16),
-        pltpu.SemaphoreType.DMA((22,)),
-        pltpu.SemaphoreType.DMA((22,)),
+        pltpu.SemaphoreType.DMA((30,)),
+        pltpu.SemaphoreType.DMA((30,)),
         pltpu.SemaphoreType.DMA((8,)),
     ]
     outs = pl.pallas_call(

time: 115 us -> 107 us (0.930)
  Pallas kernels: 111 us -> 102 us
    pallas_call x1, Pallas kernels: 111 us -> 102 us  [per_device(): pl.pallas_call(kernel, out_shape=[jax.ShapeDtypeStruct(flat, BF16)] * 3,...]
where the time goes in v3:
time: 107 us; the launch traced here: 106 us
  Pallas kernels  102 us (95%)
  local copies, waits for them, and re-layouts  3.18 us (3%)
    pallas_call x1, Pallas kernels, per_device(): pl.pallas_call(kernel, out_shape=[jax.ShapeDtypeStruct(flat, BF16)] * 3,...  102 us
    unnamed x7, local copies, waits for them, and re-layouts  3.18 us

profile of v3, /device:TPU:1, one launch (start us, length us, event | category | flops | bytes accessed | tf_op | source)
XLA Modules:
  0.0 106.3 jit_solution(12407595737208696226)
XLA Ops:
  0.6 0.0 copy-start
  0.6 0.0 copy-start.1
  0.7 0.7 copy-done
  1.3 0.0 copy-done.1
  1.3 102.5 %shard_map.85 = (bf16[128,2560]{1,0:T(8,128)(2,1)S(1)}, bf16[128,2560]{1,0:T(8,128)(2,1)S(1)}, bf16[128,2560]{1,0:T(8,128)(2,1)S(1)}) custom-call(bf16[128,2560]{1,0:T(8,128)(2,1)} %bitcast.16, bf16[128,2560]{1,0:T(8,128)(2,1)} %bitcast.17, bf16[128,2560]{1,0:T(8,128)(2,1)} %bitcast.18, bf16[128,2560]{1,0:T(8,128)(2,1)} %bitcast.19, ...), custom_call_target="tpu_custom_call" | custom-call | tf_op jit(solution)/shard_map/pallas_call | solution.py:494
  103.8 0.8 copy.15
  104.6 0.8 copy.16
  105.5 0.8 copy.17
Async XLA Ops:
  0.6 0.7 copy-start
  0.6 0.7 copy-start.1

commit v4 on v3

--- a/solution.py
+++ b/solution.py
@@ -75,8 +75,8 @@
     ms, rs, zp, zb, bp, bt, mp, mem, memk, memv,
     ms2, rs2, zp2, zb2, bp2, bt2, mp2, mem2,
     m2, dm,
-    cskv, csqg, crkv, crqg, sep, hr, hc, gs, gr, own, cown, cgs, cgr,
-    bsq, bskv, brq, brkv,
+    cskv, csq, csg, crkv, crq, crg, sep, hr, hc, gs, gr, own, cown, cgs, cgr,
+    bsq, bsk, bsv, brq, brk, brv,
     send, recv, load,
 ):
     r = lax.axis_index("row")
@@ -166,11 +166,11 @@
     to_pair = select(128, 128, by_pair)
     mine = pl.ds(pl.multiple_of(hh * PART, 128), PART)
 
-    def arrange(first, second, to):
+    def arrange(refs, to):
         def body(h, c):
             ln = pl.ds(pl.multiple_of(h * 256, 256), 256)
             wide = pl.ds(pl.multiple_of(HALF + h * 256, 256), 256)
-            for a, ref in enumerate((first, second)):
+            for a, ref in enumerate(refs):
                 to[:, a, :, ln] = dot(to_pair, ref[:, wide]).astype(BF16).reshape(8, 16, 256)
             return c
 
@@ -201,14 +201,13 @@
 
         around(visit)
 
-    arrange(k_ref, v_ref, cskv)
+    arrange((k_ref, v_ref), cskv)
     scatter(cskv, crkv, 4)
     crkv[r] = cskv[jp, :, :, mine]
-    fetch(2, 1).wait()
-    fetch(3, 1).wait()
-    arrange(q_ref, g_ref, csqg)
-    scatter(csqg, crqg, 21)
-    crqg[r] = csqg[jp, :, :, mine]
+    for a, ref, cut, to in ((2, q_ref, csq, crq), (3, g_ref, csg, crg)):
+        fetch(a, 1).wait()
+        arrange((ref,), cut)
+        to[r] = cut[jp, :, :, mine]
 
     log_rate = jnp.log(
         jnp.concatenate([jnp.full((1, 128), decay_ref[h], F32) for h in range(20)], axis=1)
@@ -255,6 +254,7 @@
     total = jnp.sum(rs[...], axis=0)
     norm = 1.0 / jnp.sqrt(jnp.maximum(total[:, FEATS : FEATS + 1], 1.0))
     to_the_block(total[:, :FEATS] * norm, zp, zb, 1)
+    scatter(csq, crq, 21)
 
     to_stripe = select(256, 256, by_stripe)
 
@@ -267,13 +267,12 @@
     arrived(crkv.at[pl.ds(0, 15)], 4)
     split(crkv, 0, 1)
     split(crkv, 1, 2)
+    inside = to_the_blocks(zb, bp, bt, 2, 0)
     push(sep.at[pl.ds(1, 2), 0], hc.at[1], 9, {"row": pair_before})
     push(sep.at[pl.ds(1, 2), 1], hc.at[0], 10, {"row": pair_after})
-
-    inside = to_the_blocks(zb, bp, bt, 2, 0)
+    scatter(csg, crg, 12)
     to_the_row(inside, bt, mp, mem, 3, 0, None)
 
-    arrived(crqg.at[pl.ds(0, 15)], 21)
     before = lax.rem(r + ROWS - 1, ROWS)
     after = lax.rem(r + 1, ROWS)
     for i in range(2):
@@ -281,8 +280,10 @@
         for a, ref in enumerate((k_ref, v_ref)):
             push(ref.at[cols], hr.at[i, 1, a], 22 + 4 * i + 2 * a, {"row": before})
             push(ref.at[cols], hr.at[i, 0, a], 23 + 4 * i + 2 * a, {"row": after})
-    split(crqg, 0, 0)
-    split(crqg, 1, 3)
+    arrived(crq.at[pl.ds(0, 15)], 21)
+    split(crq, 0, 0)
+    arrived(crg.at[pl.ds(0, 15)], 12)
+    split(crg, 0, 3)
 
     arrived(mem.at[pl.ds(0, 15)], 3)
     zero = jnp.zeros((S, FEATS), F32)
@@ -365,7 +366,6 @@
         push(gs.at[i, 1], gr.at[i, 0], 6 + 2 * i, {"row": after})
 
     row_heads(0)
-    row_back(0)
     row_heads(1)
 
     for a in range(2):
@@ -373,11 +373,11 @@
             ms2[a * S + s] = dm[a, s : s + 1, :]
     rs2[r] = ms2[r]
     push_row(lambda t: ms2.at[t], rs2.at[r], 15)
-    row_back(1)
+    row_back(0)
 
     arrived(cgr.at[1], 13)
     arrived(cgr.at[0], 14)
-    for a in range(2):
+    for a, (cut, to) in enumerate(((bsk, brk), (bsv, brv))):
         full = jnp.concatenate(
             [
                 cown[a, 0:128, :] + cgr[0, a].astype(F32),
@@ -385,14 +385,16 @@
             ],
             axis=0,
         ).astype(BF16)
-        bskv[:, a, :, :] = dot(from_stripe, full).astype(BF16).reshape(16, 16, PART)
-    brkv[jp, :, :, mine] = bskv[r]
-    push_row(lambda t: bskv.at[t], brkv.at[jp, :, :, mine], 20)
+        cut[...] = dot(from_stripe, full).astype(BF16).reshape(16, 16, PART)
+        to[jp, :, mine] = cut[r]
 
     arrived(rs2.at[pl.ds(0, 15)], 15)
     to_the_block(jnp.sum(rs2[...], axis=0), zp2, zb2, 16)
+    push_row(lambda t: bsk.at[t], brk.at[jp, :, mine], 20)
     inside = to_the_blocks(zb2, bp2, bt2, 17, 20)
+    push_row(lambda t: bsv.at[t], brv.at[jp, :, mine], 11)
     to_the_row(inside, bt2, mp2, mem2, 18, 20, norm)
+    row_back(1)
 
     from_pair = select_back(128, 128, by_pair)
     arrived(bsq.at[pl.ds(0, 15)], 19)
@@ -416,13 +418,14 @@
     for a in range(2):
         for s in range(S):
             dm[a, s : s + 1, :] = mem2[a * S + s]
-    arrived(bskv.at[pl.ds(0, 15)], 20)
+    arrived(bsk.at[pl.ds(0, 15)], 20)
+    arrived(bsv.at[pl.ds(0, 15)], 11)
 
     def finish(h, c):
         ln = pl.ds(pl.multiple_of(h * 256, 256), 256)
         wide = pl.ds(pl.multiple_of(HALF + h * 256, 256), 256)
-        for a, out in enumerate((ok_ref, ov_ref)):
-            back = dot(from_pair, brkv[:, a, :, ln].reshape(128, 256))
+        for a, (from_, out) in enumerate(((brk, ok_ref), (brv, ov_ref))):
+            back = dot(from_pair, from_[:, :, ln].reshape(128, 256))
             dr = dm[a, :, ln].astype(BF16)
             dc = dm[a, :, wide].astype(BF16)
             add_r = jnp.concatenate([dot(member_b[f], dr, 0, 0) for f in range(2)], axis=0)
@@ -438,7 +441,8 @@
     left(bt.at[pl.ds(0, 3)], 2)
     left(mem.at[pl.ds(0, 15)], 3)
     left(crkv.at[pl.ds(0, 15)], 4)
-    left(crqg.at[pl.ds(0, 15)], 21)
+    left(crq.at[pl.ds(0, 15)], 21)
+    left(crg.at[pl.ds(0, 15)], 12)
     for k in range(8):
         left(hr.at[0, 0, 0], 22 + k)
     for k in range(4):
@@ -452,7 +456,8 @@
     left(bt2.at[pl.ds(0, 3)], 17)
     left(mem2.at[pl.ds(0, 15)], 18)
     left(bsq.at[pl.ds(0, 15)], 19)
-    left(bskv.at[pl.ds(0, 15)], 20)
+    left(bsk.at[pl.ds(0, 15)], 20)
+    left(bsv.at[pl.ds(0, 15)], 11)
 
 
 def per_device(queries, keys, values, out_grad, slots, decay):
@@ -471,9 +476,11 @@
         row(1), row(8), row(1), row(4), row(1), row(16),
         pltpu.VMEM((16, FEATS), F32), pltpu.VMEM((2, S, FEATS), F32),
         pltpu.VMEM((8, 2, 16, HALF), BF16),
-        pltpu.VMEM((8, 2, 16, HALF), BF16),
+        pltpu.VMEM((8, 1, 16, HALF), BF16),
+        pltpu.VMEM((8, 1, 16, HALF), BF16),
         pltpu.VMEM((16, 2, 16, PART), BF16),
-        pltpu.VMEM((16, 2, 16, PART), BF16),
+        pltpu.VMEM((16, 1, 16, PART), BF16),
+        pltpu.VMEM((16, 1, 16, PART), BF16),
         pltpu.VMEM((4, 2, 128, PART), BF16),
         pltpu.VMEM((2, 2, 2, 128, PART), BF16),
         pltpu.VMEM((2, 2, 128, PART), BF16),
@@ -483,10 +490,8 @@
         pltpu.VMEM((2, 256, PART), F32),
         pltpu.VMEM((2, 2, 128, PART), BF16),
         pltpu.VMEM((2, 2, 128, PART), BF16),
-        pltpu.VMEM((16, 16, PART), BF16),
-        pltpu.VMEM((16, 2, 16, PART), BF16),
-        pltpu.VMEM((8, 16, HALF), BF16),
-        pltpu.VMEM((8, 2, 16, HALF), BF16),
+        *[pltpu.VMEM((16, 16, PART), BF16)] * 3,
+        *[pltpu.VMEM((8, 16, HALF), BF16)] * 3,
         pltpu.SemaphoreType.DMA((30,)),
         pltpu.SemaphoreType.DMA((30,)),
         pltpu.SemaphoreType.DMA((8,)),

time: 107 us -> 105 us (0.981)
    pallas_call x1, Pallas kernels: 102 us -> 101 us  [per_device(): pl.pallas_call(kernel, out_shape=[jax.ShapeDtypeStruct(flat, BF16)] * 3,...]
where the time goes in v4:
time: 105 us
  Pallas kernels  101 us (96%)
  local copies, waits for them, and re-layouts  3.18 us (3%)
    pallas_call x1, Pallas kernels, per_device(): pl.pallas_call(kernel, out_shape=[jax.ShapeDtypeStruct(flat, BF16)] * 3,...  101 us
    unnamed x7, local copies, waits for them, and re-layouts  3.18 us

profile of v4, /device:TPU:1, one launch (start us, length us, event | category | flops | bytes accessed | tf_op | source)
XLA Modules:
  0.0 105.0 jit_solution(12116365760978980427)
XLA Ops:
  0.6 0.0 copy-start
  0.6 0.0 copy-start.1
  0.7 0.7 copy-done
  1.3 0.0 copy-done.1
  1.3 101.2 %shard_map.85 = (bf16[128,2560]{1,0:T(8,128)(2,1)S(1)}, bf16[128,2560]{1,0:T(8,128)(2,1)S(1)}, bf16[128,2560]{1,0:T(8,128)(2,1)S(1)}) custom-call(bf16[128,2560]{1,0:T(8,128)(2,1)} %bitcast.16, bf16[128,2560]{1,0:T(8,128)(2,1)} %bitcast.17, bf16[128,2560]{1,0:T(8,128)(2,1)} %bitcast.18, bf16[128,2560]{1,0:T(8,128)(2,1)} %bitcast.19, ...), custom_call_target="tpu_custom_call" | custom-call | tf_op jit(solution)/shard_map/pallas_call | solution.py:499
  102.5 0.8 copy.15
  103.4 0.8 copy.16
  104.2 0.8 copy.17
Async XLA Ops:
  0.6 0.7 copy-start
  0.6 0.7 copy-start.1

commit v5 on v4

--- a/solution.py
+++ b/solution.py
@@ -69,9 +69,9 @@
 
 
 def kernel(
-    qh_ref, kh_ref, vh_ref, gh_ref, slots_ref, decay_ref,
+    qh_ref, kh_ref, vh_ref, gh_ref, slots_h_ref, decay_h_ref,
     oq_ref, ok_ref, ov_ref,
-    q_ref, k_ref, v_ref, g_ref, wts,
+    q_ref, k_ref, v_ref, g_ref, slots_ref, decay_ref, wts,
     ms, rs, zp, zb, bp, bt, mp, mem, memk, memv,
     ms2, rs2, zp2, zb2, bp2, bt2, mp2, mem2,
     m2, dm,
@@ -136,6 +136,11 @@
         for part in (1, 0):
             fetch(a, part).start()
 
+    fetch_slots = pltpu.make_async_copy(slots_h_ref, slots_ref, load.at[8])
+    fetch_decay = pltpu.make_async_copy(decay_h_ref, decay_ref, load.at[9])
+    fetch_slots.start()
+    fetch_decay.start()
+
     def push(src, dst, k, device):
         pltpu.make_async_remote_copy(
             src_ref=src, dst_ref=dst, send_sem=send.at[k], recv_sem=recv.at[k],
@@ -176,6 +181,8 @@
 
         lax.fori_loop(0, 5, body, 0)
 
+    fetch_slots.wait()
+    fetch_decay.wait()
     for part in range(2):
         for a in range(2):
             fetch(a, part).wait()
@@ -326,13 +333,12 @@
         sep[0, 1, :, ln] = qb.astype(BF16)
         return c
 
-    lax.fori_loop(0, 5, col_head, 0)
+    lax.fori_loop(0, 5, col_head, 0, unroll=True)
     push(cgs.at[0], cgr.at[1], 13, {"row": pair_before})
     push(cgs.at[1], cgr.at[0], 14, {"row": pair_after})
     from_stripe = select_back(256, 256, by_stripe)
     bsq[...] = dot(from_stripe, sep[0].reshape(256, PART)).astype(BF16).reshape(16, 16, PART)
     brq[jp, :, mine] = bsq[r]
-    push_row(lambda t: bsq.at[t], brq.at[jp, :, mine], 19)
 
     row_low = jnp.where(r > 0, 0.0, NEG)
     row_high = jnp.where(r < ROWS - 1, 0.0, NEG)
@@ -359,7 +365,7 @@
                 dm[a, :, ln] = d[384:392]
             return c
 
-        lax.fori_loop(0, 5, body, 0)
+        lax.fori_loop(0, 5, body, 0, unroll=True)
 
     def row_back(i):
         push(gs.at[i, 0], gr.at[i, 1], 5 + 2 * i, {"row": before})
@@ -374,6 +380,7 @@
     rs2[r] = ms2[r]
     push_row(lambda t: ms2.at[t], rs2.at[r], 15)
     row_back(0)
+    push_row(lambda t: bsq.at[t], brq.at[jp, :, mine], 19)
 
     arrived(cgr.at[1], 13)
     arrived(cgr.at[0], 14)
@@ -468,7 +475,8 @@
         return pltpu.VMEM((count, 1, width), F32)
 
     scratch = [
-        *[pltpu.VMEM(flat, BF16)] * 4, row(40),
+        *[pltpu.VMEM(flat, BF16)] * 4,
+        pltpu.VMEM(slots.shape, jnp.int32), pltpu.SMEM(decay.shape, F32), row(40),
         row(16, FEATS + 128), row(16, FEATS + 128),
         row(1), row(8), row(1), row(4), row(1), row(16),
         pltpu.VMEM((16, FEATS), BF16), pltpu.VMEM((16, FEATS), BF16),
@@ -494,12 +502,12 @@
         *[pltpu.VMEM((8, 16, HALF), BF16)] * 3,
         pltpu.SemaphoreType.DMA((30,)),
         pltpu.SemaphoreType.DMA((30,)),
-        pltpu.SemaphoreType.DMA((8,)),
+        pltpu.SemaphoreType.DMA((10,)),
     ]
     outs = pl.pallas_call(
         kernel,
         out_shape=[jax.ShapeDtypeStruct(flat, BF16)] * 3,
-        in_specs=[pl.BlockSpec(memory_space=pltpu.HBM)] * 4 + [vm] + [pl.BlockSpec(memory_space=pltpu.SMEM)],
+        in_specs=[pl.BlockSpec(memory_space=pltpu.HBM)] * 6,
         out_specs=[vm] * 3,
         scratch_shapes=scratch,
         compiler_params=pltpu.CompilerParams(
@@ -507,10 +515,12 @@
         ),
     )(
         *[
-            pltpu.with_memory_space_constraint(a.reshape(flat), pltpu.HBM)
-            for a in (queries, keys, values, out_grad)
+            pltpu.with_memory_space_constraint(a, pltpu.HBM)
+            for a in (
+                queries.reshape(flat), keys.reshape(flat), values.reshape(flat),
+                out_grad.reshape(flat), slots, decay,
+            )
         ],
-        slots, decay,
     )
     return tuple(o.reshape(queries.shape) for o in outs)
 

time: 105 us -> 102 us (0.971)
  Pallas kernels: 101 us -> 98.6 us
    pallas_call x1, Pallas kernels: 101 us -> 98.6 us  [per_device(): pl.pallas_call(kernel, out_shape=[jax.ShapeDtypeStruct(flat, BF16)] * 3,...]
    unnamed x7 -> x3, local copies, waits for them, and re-layouts: 3.18 us -> 2.51 us
where the time goes in v5:
time: 102 us
  Pallas kernels  98.6 us (97%)
  local copies, waits for them, and re-layouts  2.51 us (2%)
    pallas_call x1, Pallas kernels, per_device(): pl.pallas_call(kernel, out_shape=[jax.ShapeDtypeStruct(flat, BF16)] * 3,...  98.6 us
    unnamed x3, local copies, waits for them, and re-layouts  2.51 us

profile of v5, /device:TPU:1, one launch (start us, length us, event | category | flops | bytes accessed | tf_op | source)
XLA Modules:
  0.0 101.8 jit_solution(9760512945065462219)
XLA Ops:
  0.6 98.6 %shard_map.85 = (bf16[128,2560]{1,0:T(8,128)(2,1)S(1)}, bf16[128,2560]{1,0:T(8,128)(2,1)S(1)}, bf16[128,2560]{1,0:T(8,128)(2,1)S(1)}) custom-call(bf16[128,2560]{1,0:T(8,128)(2,1)} %bitcast.16, bf16[128,2560]{1,0:T(8,128)(2,1)} %bitcast.17, bf16[128,2560]{1,0:T(8,128)(2,1)} %bitcast.18, bf16[128,2560]{1,0:T(8,128)(2,1)} %bitcast.19, ...), custom_call_target="tpu_custom_call" | custom-call | tf_op jit(solution)/shard_map/pallas_call | solution.py:507
  99.2 0.8 copy.15
  100.1 0.8 copy.16
  100.9 0.8 copy.17
